TPU v7x, 128 devices: a whole 4x4x4 slice. The times are simulated.
128 devices in a mesh: rep: 8 (over z, y_hi), tp: 16 (over y_lo, x, core).
Axes of the slice: x: 4, y: 4 (y_hi: 2, y_lo: 2; y = y_hi * 2 + y_lo), z: 4, core: 2. Of those that a mesh axis runs over, the one named last changes fastest.
Arguments:
- tokens: bfloat16 [8192, 2560], P('rep', 'tp'), may hold values from -6 to 6
- output_grads: bfloat16 [8192, 14336], P('rep', 'tp'), may hold values from -6 to 6
- momentum: bfloat16 [8, 2560, 14336], P('rep', None, 'tp'), may hold values from -1.1953125 to 1.1953125
- component_picks: int32 [8, 40, 224, 32], P(None, None, 'tp'), may hold values from 0 to 4095, as said below
Outputs:
- new_momentum: bfloat16 [8, 2560, 14336], P('rep', None, 'tp')
- update: bfloat16 [2560, 14336], P(None, 'tp')
Inputs may be any that keep to these rules, and one draw needn't show every extreme that they name: `component_picks`: pick k of each block lies in k * 128 to (k + 1) * 128 - 1, so the picks of one block are distinct.
All inputs are finite; a program needn't handle non-finite values.
Results may differ from a plain program's by a relative error of at most 0.001.
Values may be sent and summed in bfloat16 or wider, within the bound.
A program may use at most 256 MiB of HBM per device.

v0:
```python
import math

import jax
import jax.numpy as jnp
from jax import lax
from jax.sharding import PartitionSpec as P

ROWS = 1024
BLOCK = 64


DECAY = 0.9
EPSILON = 1e-06
PRECISE = lax.Precision.HIGHEST


def cosine_table():
    frequency = jnp.arange(BLOCK, dtype=jnp.float32)[:, None]
    position = jnp.arange(BLOCK, dtype=jnp.float32)[None, :]
    weights_norm = jnp.where(frequency == 0, math.sqrt(1.0 / BLOCK), math.sqrt(2.0 / BLOCK))
    return weights_norm * jnp.cos(math.pi * (2.0 * position + 1.0) * frequency / (2.0 * BLOCK))


def forward_blocks(grid_in, cosine):
    row_total, col_total = grid_in.shape
    tiles = grid_in.reshape(row_total // BLOCK, BLOCK, col_total // BLOCK, BLOCK)
    halfway = jnp.einsum("ai,pibj->pabj", cosine, tiles, precision=PRECISE)
    return jnp.einsum("pabj,cj->pabc", halfway, cosine, precision=PRECISE)


def backward_blocks(tiles, cosine):
    block_rows, _, block_cols, _ = tiles.shape
    halfway = jnp.einsum("ai,pabc->pibc", cosine, tiles, precision=PRECISE)
    result = jnp.einsum("pibc,cj->pibj", halfway, cosine, precision=PRECISE)
    return result.reshape(block_rows * BLOCK, block_cols * BLOCK)


def slot_mask(picks):
    ordered = jnp.transpose(picks, (0, 2, 1))
    within = ordered % (2 * BLOCK)
    half_row = (within // BLOCK)[:, :, None, :, None]
    column = (within % BLOCK)[:, :, None, :, None]
    half_iota = jnp.arange(2, dtype=jnp.int32)[None, None, :, None, None]
    col_iota = jnp.arange(BLOCK, dtype=jnp.int32)[None, None, None, None, :]
    return (half_iota == half_row) & (col_iota == column)


def as_slots(tiles):
    block_rows, _, block_cols, _ = tiles.shape
    return tiles.reshape(block_rows, BLOCK // 2, 2, block_cols, BLOCK)


def spread_values(masks, picked):
    ordered = jnp.transpose(picked, (0, 2, 1))[:, :, None, :, None]
    return jnp.where(masks, ordered, 0.0)


def block_rescale(summed):
    row_total, col_total = summed.shape
    tiles = summed.reshape(row_total // BLOCK, BLOCK, col_total // BLOCK, BLOCK)
    mean_square = jnp.mean(tiles * tiles, axis=(1, 3), keepdims=True)
    return (tiles * lax.rsqrt(mean_square + EPSILON)).reshape(row_total, col_total)


def body(tokens, output_grads, momentum, component_picks):
    cosine = cosine_table()
    row_total = momentum.shape[1]
    col_count = momentum.shape[2]
    block_rows = row_total // BLOCK
    block_cols = col_count // BLOCK
    group_count = lax.axis_size("rep")
    group_index = lax.axis_index("rep")
    gradient = lax.dot_general(
        lax.all_gather(tokens, "tp", axis=1, tiled=True),
        output_grads,
        (((0,), (0,)), ((), ())),
        preferred_element_type=jnp.float32,
    )
    moved = DECAY * momentum[0].astype(jnp.float32) + gradient * (1.0 / math.sqrt(ROWS))
    slots = as_slots(forward_blocks(moved, cosine))
    own_picks = lax.dynamic_index_in_dim(component_picks, group_index, 0, keepdims=False)
    own_mask = slot_mask(own_picks)
    values = jnp.transpose(jnp.sum(jnp.where(own_mask, slots, 0.0), axis=(2, 4)), (0, 2, 1))
    remaining = jnp.where(own_mask, 0.0, slots).reshape(block_rows, BLOCK, block_cols, BLOCK)
    new_momentum = backward_blocks(remaining, cosine).astype(jnp.bfloat16)
    gathered = lax.all_gather(values[None], "rep", axis=0, tiled=True)
    dense_slots = jnp.zeros(slots.shape, jnp.float32)
    for member in range(group_count):
        dense_slots = dense_slots + spread_values(
            slot_mask(component_picks[member]), gathered[member]
        )
    summed = backward_blocks(dense_slots.reshape(block_rows, BLOCK, block_cols, BLOCK), cosine)
    update = block_rescale(summed).astype(jnp.bfloat16)
    return (new_momentum[None], update)


def solution(mesh):
    return jax.shard_map(
        body,
        mesh=mesh,
        in_specs=(P("rep", "tp"), P("rep", "tp"), P("rep", None, "tp"), P(None, None, "tp", None)),
        out_specs=(P("rep", None, "tp"), P(None, "tp")),
        check_vma=False,
    )
```

profile of v0, /device:TPU:1, one launch (start us, length us, event | category | flops | bytes accessed | tf_op | source)
XLA Modules:
  0.0 555.4 jit_solution(1653650667171583593)
XLA Ops:
  7.9 5.2 add_select_fusion.22
  18.3 10.4 %copy.171 = pred[40,64,14,64]{1,3,2,0:T(32,128)(4,1)} copy(pred[40,64,14,64]{3,0,2,1:T(8,128)(4,1)S(1)} %bitcast.172) | data formatting | bytes 4587520 | tf_op jit(solution)/shard_map/and | solution.py:45
  45.5 10.4 %copy.216 = pred[40,64,14,64]{1,3,2,0:T(32,128)(4,1)} copy(pred[40,64,14,64]{3,0,2,1:T(8,128)(4,1)S(1)} %bitcast.173) | data formatting | bytes 4587520 | tf_op jit(solution)/shard_map/and | solution.py:45
  60.9 10.4 %copy.211 = pred[40,64,14,64]{1,3,2,0:T(32,128)(4,1)} copy(pred[40,64,14,64]{3,0,2,1:T(8,128)(4,1)S(1)} %bitcast.174) | data formatting | bytes 4587520 | tf_op jit(solution)/shard_map/and | solution.py:45
  76.5 10.4 %copy.206 = pred[40,64,14,64]{1,3,2,0:T(32,128)(4,1)} copy(pred[40,64,14,64]{3,0,2,1:T(8,128)(4,1)S(1)} %bitcast.175) | data formatting | bytes 4587520 | tf_op jit(solution)/shard_map/and | solution.py:45
  91.9 10.4 %copy.201 = pred[40,64,14,64]{1,3,2,0:T(32,128)(4,1)} copy(pred[40,64,14,64]{3,0,2,1:T(8,128)(4,1)S(1)} %bitcast.176) | data formatting | bytes 4587520 | tf_op jit(solution)/shard_map/and | solution.py:45
  107.3 10.3 %copy.196 = pred[40,64,14,64]{1,3,2,0:T(32,128)(4,1)} copy(pred[40,64,14,64]{3,0,2,1:T(8,128)(4,1)S(1)} %bitcast.177) | data formatting | bytes 4587520 | tf_op jit(solution)/shard_map/and | solution.py:45
  122.6 10.8 %copy.191 = pred[40,64,14,64]{1,3,2,0:T(32,128)(4,1)} copy(pred[40,64,14,64]{3,0,2,1:T(8,128)(4,1)S(1)} %bitcast.178) | data formatting | bytes 4587520 | tf_op jit(solution)/shard_map/and | solution.py:45
  138.4 10.4 %copy.186 = pred[40,64,14,64]{1,3,2,0:T(32,128)(4,1)} copy(pred[40,64,14,64]{3,0,2,1:T(8,128)(4,1)S(1)} %bitcast.179) | data formatting | bytes 4587520 | tf_op jit(solution)/shard_map/and | solution.py:45
  153.9 10.4 %copy.179 = pred[40,64,14,64]{1,3,2,0:T(32,128)(4,1)} copy(pred[40,64,14,64]{3,0,2,1:T(8,128)(4,1)S(1)} %bitcast.180) | data formatting | bytes 4587520 | tf_op jit(solution)/shard_map/and | solution.py:45
  171.3 11.8 %bitcast_add_fusion = f32[2560,896]{1,0:T(8,128)} fusion(bf16[1,2560,896]{2,1,0:T(8,128)(2,1)} %param.6, bf16[1024,2560]{0,1:T(8,128)(2,1)} %all-gather.3.cloned.1.call-done, bf16[1024,896]{1,0:T(8,128)(2,1)S(1)} %copy-done), kind=kOutput, calls=%fused_computation.38 | convolution fusion | flops 4706795520 | bytes 20840448 | tf_op jit(solution)/shard_map/dot_general | solution.py:73
  183.0 15.8 %reshape.256 = f32[40,64,14,64]{3,2,1,0:T(8,128)} reshape(f32[2560,896]{1,0:T(8,128)} %bitcast_add_fusion) | data formatting | bytes 18350080 | tf_op jit(solution)/shard_map/reshape | solution.py:26
  198.9 38.8 %fusion.6 = f32[40,14,64,64]{3,2,1,0:T(8,128)} fusion(f32[40,64,14,64]{3,2,1,0:T(8,128)} %reshape.256, f32[64]{0:T(128)S(1)} %get-tuple-element.50, f32[64]{0:T(128)S(1)} %get-tuple-element.49), kind=kOutput, calls=%fused_computation.6 | convolution fusion | flops 1761619968 | bytes 18350592 | tf_op jit(solution)/shard_map/ai,pibj->pabj/dot_general | solution.py:27
  237.6 29.1 %select_reduce_fusion = (f32[40,64,14]{1,2,0:T(8,128)S(1)}, f32[40,64,14,64]{1,3,2,0:T(8,128)}) fusion(pred[40,64,14,64]{1,3,2,0:T(32,128)(4,1)} %copy.171, pred[40,64,14]{1,2,0:T(8,128)(4,1)S(1)} %copy.169, f32[64]{0:T(128)S(1)} %get-tuple-element.50, f32[64]{0:T(128)S(1)} %get-tuple-element.49, f32[40,14,64,64]{3,2,1,0:T(8,128)} %fusion.6), kind=kOutput, calls=%fused_computation.26 | convolution fusion | flops 1768465408 | bytes 20823552 | tf_op jit(solution)/shard_map/pabj,cj->pabc/dot_general | solution.py:28
  266.7 20.9 %fusion.24 = f32[40,14,64,64]{3,2,1,0:T(8,128)S(1)} fusion(f32[40,64,14,64]{1,3,2,0:T(8,128)} %get-tuple-element.46, pred[40,64,14,64]{1,3,2,0:T(32,128)(4,1)} %copy.171, pred[40,64,14]{1,2,0:T(8,128)(4,1)S(1)} %copy.169, f32[64]{0:T(128)S(1)} %get-tuple-element.50, f32[64]{0:T(128)S(1)} %get-tuple-element.49), kind=kOutput, calls=%fused_computation.27 | convolution fusion | flops 1766207488 | bytes 20680192 | tf_op jit(solution)/shard_map/ai,pabc->pibc/dot_general | solution.py:33
  287.7 31.6 %fusion.54 = bf16[40,64,14,64]{3,1,2,0:T(8,128)(2,1)} fusion(f32[40,14,64,64]{3,2,1,0:T(8,128)S(1)} %fusion.24, f32[64]{0:T(128)S(1)} %get-tuple-element.50, f32[64]{0:T(128)S(1)} %get-tuple-element.49), kind=kOutput, calls=%fused_computation.67 | convolution fusion | flops 1763913728 | bytes 13763072 | tf_op jit(solution)/shard_map/pibc,cj->pibj/dot_general | solution.py:34
  319.3 25.8 %copy.229 = bf16[40,64,14,64]{3,2,1,0:T(8,128)(2,1)} copy(bf16[40,64,14,64]{3,1,2,0:T(8,128)(2,1)} %fusion.54) | data formatting | bytes 9175040
  345.1 14.0 %reshape.257 = bf16[1,2560,896]{2,1,0:T(8,128)(2,1)} reshape(bf16[40,64,14,64]{3,2,1,0:T(8,128)(2,1)} %copy.229) | data formatting | bytes 9175040
  360.1 57.2 %all-gather = f32[320,14,32]{2,1,0:T(8,128)S(1)} all-gather(f32[40,14,32]{2,1,0:T(8,128)S(1)} %copy.181), channel_id=2, replica_groups=mesh['rep'=8,'tp'=16] {'rep'}, dimensions={0}, use_global_device_ids=true | all-gather | bytes 645120 | tf_op jit(solution)/shard_map/all_gather | solution.py:86
  423.5 43.5 %fusion.8 = f32[40,14,64,64]{3,2,1,0:T(8,128)} fusion(pred[40,64,14,64]{1,3,2,0:T(32,128)(4,1)} %copy.216, pred[40,64,14,64]{1,3,2,0:T(32,128)(4,1)} %copy.211, pred[40,64,14,64]{1,3,2,0:T(32,128)(4,1)} %copy.206, pred[40,64,14,64]{1,3,2,0:T(32,128)(4,1)} %copy.201, pred[40,64,14,64]{1,3,2,0:T(32,128)(4,1)} %copy.196, pred[40,64,14,64]{1,3,2,0:T(32,128)(4,1)} %copy.191, ...), kind=kOutput, calls=%fused_computation.10 | convolution fusion | flops 1814376448 | bytes 28959232 | tf_op jit(solution)/shard_map/ai,pabc->pibc/dot_general | solution.py:33
  467.1 36.6 %multiply_reduce_fusion = (f32[40,14]{1,0:T(8,128)S(1)}, f32[40,64,14,64]{3,1,2,0:T(8,128)S(1)}) fusion(f32[64]{0:T(128)S(1)} %get-tuple-element.50, f32[64]{0:T(128)S(1)} %get-tuple-element.49, f32[40,14,64,64]{3,2,1,0:T(8,128)} %fusion.8), kind=kOutput, calls=%fused_computation.9 | convolution fusion | flops 1766206976 | bytes 18352832 | tf_op jit(solution)/shard_map/pibc,cj->pibj/dot_general | solution.py:34
  503.6 4.7 multiply_convert_fusion
  508.4 25.9 %copy.230 = bf16[40,64,14,64]{3,2,1,0:T(8,128)(2,1)} copy(bf16[40,64,14,64]{3,1,2,0:T(8,128)(2,1)} %multiply_convert_fusion) | data formatting | bytes 9175040
  534.3 14.0 %reshape.258 = bf16[2560,896]{1,0:T(8,128)(2,1)} reshape(bf16[40,64,14,64]{3,2,1,0:T(8,128)(2,1)} %copy.230) | data formatting | bytes 9175040
  (111 shorter events, 72.0 us)
Async XLA Ops:
  7.2 164.1 %copy-start = (bf16[1024,896]{1,0:T(8,128)(2,1)S(1)}, bf16[1024,896]{1,0:T(8,128)(2,1)}, u32[]{:S(2)}) copy-start(bf16[1024,896]{1,0:T(8,128)(2,1)} %param.5) | copy-start | bytes 5505028
  7.2 164.1 %all-gather.3.cloned.1.call-start = ((), (), s32[]{:S(2)}) async-start(), calls=%async_computation | async-start | bytes 5570560 | tf_op jit(solution)/shard_map/all_gather | solution.py:74
  28.7 7.9 %copy-start.3 = (s32[40,32,14]{0,1,2:T(8,128)S(1)}, s32[40,32,14]{0,1,2:T(8,128)}, u32[]{:S(2)}) copy-start(s32[40,32,14]{0,1,2:T(8,128)} %get-tuple-element.34) | copy-start | bytes 215044
  28.7 8.0 %copy-start.2 = (s32[40,32,14]{0,1,2:T(8,128)S(1)}, s32[40,32,14]{0,1,2:T(8,128)}, u32[]{:S(2)}) copy-start(s32[40,32,14]{0,1,2:T(8,128)} %get-tuple-element.33) | copy-start | bytes 215044
  153.8 10.5 %copy-start.11 = (pred[40,64,14]{0,1,2:T(8,128)(4,1)S(1)}, pred[40,64,14]{0,1,2:T(8,128)(4,1)}, u32[]{:S(2)}) copy-start(pred[40,64,14]{0,1,2:T(8,128)(4,1)} %get-tuple-element.43) | copy-start | bytes 107524
  153.8 11.4 %copy-start.10 = (pred[40,64,14]{0,1,2:T(8,128)(4,1)S(1)}, pred[40,64,14]{0,1,2:T(8,128)(4,1)}, u32[]{:S(2)}) copy-start(pred[40,64,14]{0,1,2:T(8,128)(4,1)} %get-tuple-element.42) | copy-start | bytes 107524
  153.8 12.2 %copy-start.9 = (pred[40,64,14]{0,1,2:T(8,128)(4,1)S(1)}, pred[40,64,14]{0,1,2:T(8,128)(4,1)}, u32[]{:S(2)}) copy-start(pred[40,64,14]{0,1,2:T(8,128)(4,1)} %get-tuple-element.41) | copy-start | bytes 107524
  153.8 13.1 %copy-start.8 = (pred[40,64,14]{0,1,2:T(8,128)(4,1)S(1)}, pred[40,64,14]{0,1,2:T(8,128)(4,1)}, u32[]{:S(2)}) copy-start(pred[40,64,14]{0,1,2:T(8,128)(4,1)} %get-tuple-element.40) | copy-start | bytes 107524
  153.9 13.9 %copy-start.7 = (pred[40,64,14]{0,1,2:T(8,128)(4,1)S(1)}, pred[40,64,14]{0,1,2:T(8,128)(4,1)}, u32[]{:S(2)}) copy-start(pred[40,64,14]{0,1,2:T(8,128)(4,1)} %get-tuple-element.39) | copy-start | bytes 107524
  153.9 14.8 %copy-start.6 = (pred[40,64,14]{0,1,2:T(8,128)(4,1)S(1)}, pred[40,64,14]{0,1,2:T(8,128)(4,1)}, u32[]{:S(2)}) copy-start(pred[40,64,14]{0,1,2:T(8,128)(4,1)} %get-tuple-element.38) | copy-start | bytes 107524
  153.9 15.7 %copy-start.5 = (pred[40,64,14]{0,1,2:T(8,128)(4,1)S(1)}, pred[40,64,14]{0,1,2:T(8,128)(4,1)}, u32[]{:S(2)}) copy-start(pred[40,64,14]{0,1,2:T(8,128)(4,1)} %get-tuple-element.37) | copy-start | bytes 107524
  153.9 16.5 %copy-start.4 = (pred[40,64,14]{0,1,2:T(8,128)(4,1)S(1)}, pred[40,64,14]{0,1,2:T(8,128)(4,1)}, u32[]{:S(2)}) copy-start(pred[40,64,14]{0,1,2:T(8,128)(4,1)} %get-tuple-element.36) | copy-start | bytes 107524
  419.5 3.9 copy-start.13
  419.6 3.9 copy-start.14
  421.4 2.1 copy-start.12
  508.3 40.0 %copy-start.1 = (bf16[1024,896]{1,0:T(8,128)(2,1)S(1)}, bf16[1024,896]{1,0:T(8,128)(2,1)}, u32[]{:S(2)}) copy-start(bf16[1024,896]{1,0:T(8,128)(2,1)} %param.5) | copy-start | bytes 5505028
Sparse Core Ops, SparseCore 0:
  9.7 42.8 all-gather.2
where the time goes:
time: 561 us; the launch traced here: 555 us
  local copies, waits for them, and re-layouts  225 us (40%)
  matrix products  212 us (38%)
  blocking collectives  57.2 us (10%)
  other arithmetic  45.3 us (8%)
  between operations  14.8 us (3%)
    and x18, local copies, waits for them, and re-layouts, slot_mask(): return (half_iota == half_row) & (col_iota == column)  104 us
    unnamed x34, local copies, waits for them, and re-layouts  79.8 us
    dot_general x2, matrix products, backward_blocks(): result = jnp.einsum('pibc,cj->pibj', halfway, cosine, precision=PRECISE)  68.2 us
    dot_general x2, matrix products, backward_blocks(): halfway = jnp.einsum('ai,pabc->pibc', cosine, tiles, precision=PRECISE)  64.5 us
    all_gather x1, blocking collectives, body(): gathered = lax.all_gather(values[None], 'rep', axis=0, tiled=True)  57.2 us
    dot_general x1, matrix products, forward_blocks(): halfway = jnp.einsum('ai,pibj->pabj', cosine, tiles, precision=PRECISE)  38.8 us
    eq x10, other arithmetic, slot_mask(): return (half_iota == half_row) & (col_iota == column)  34.9 us
    dot_general x1, matrix products, forward_blocks(): return jnp.einsum('pabj,cj->pabc', halfway, cosine, precision=PRECISE)  29.1 us
  transfers between devices with their start and end apart: 1, of which 0 were waited for; matrix products, arithmetic and copies ran while one was open for 29% of the time, Pallas kernels for 0%

commit v1 on v0

v1 whole, which is shorter than its diff:
```python
import functools
import math

import jax
import jax.numpy as jnp
import ml_dtypes
import numpy as np
from jax import lax
from jax.experimental import pallas as pl
from jax.experimental.pallas import tpu as pltpu
from jax.sharding import PartitionSpec as P

ROWS = 1024
BLOCK = 64
HALF = 32
FIVE = 5
CHUNK = FIVE * BLOCK
LANES = 128
DECAY = 0.9
EPSILON = 1e-06
BF = jnp.bfloat16
F32 = jnp.float32


def split_table(table):
    high = table.astype(ml_dtypes.bfloat16)
    low = (table - high.astype(np.float64)).astype(ml_dtypes.bfloat16)
    return high, low


def tables(width):
    frequency = np.arange(BLOCK, dtype=np.float64)[:, None]
    position = np.arange(BLOCK, dtype=np.float64)[None, :]
    norm = np.where(frequency == 0, math.sqrt(1.0 / BLOCK), math.sqrt(2.0 / BLOCK))
    cosine = norm * np.cos(math.pi * (2.0 * position + 1.0) * frequency / (2.0 * BLOCK))
    ordered = np.concatenate([cosine[0::2], cosine[1::2]])

    def rows_table(matrix):
        high, low = split_table(matrix)
        return np.concatenate([high, high, low], axis=1)

    def lanes_table(matrix):
        pair = np.zeros((LANES, LANES))
        pair[:BLOCK, :BLOCK] = matrix
        pair[BLOCK:, BLOCK:] = matrix
        high, low = split_table(pair)
        return np.concatenate(
            [np.concatenate([high, low], axis=1), np.concatenate([high, np.zeros_like(low)], axis=1)]
        )

    slot = np.arange(LANES)[:, None] % 16
    block = np.arange(width)[None, :] // BLOCK
    expand = (slot == block).astype(ml_dtypes.bfloat16)
    same = (np.arange(LANES)[:, None] // BLOCK == np.arange(LANES)[None, :] // BLOCK).astype(ml_dtypes.bfloat16)
    return {
        "row_fwd": rows_table(ordered),
        "row_inv": rows_table(ordered.T),
        "lane_fwd": lanes_table(cosine.T),
        "lane_inv": lanes_table(cosine),
        "expand": expand,
        "expand2": np.concatenate([expand, expand]),
        "compress": np.ascontiguousarray(expand.T),
        "same": same,
    }


def dot(a, b):
    return jnp.dot(a, b, preferred_element_type=F32)


def split(value):
    high = value.astype(BF)
    return high, (value - high.astype(F32)).astype(BF)


def lane_transform(high, low, weights):
    groups = high.shape[1] // LANES
    parts = []
    for group in range(groups):
        cut = slice(group * LANES, (group + 1) * LANES)
        both = dot(jnp.concatenate([high[:, cut], low[:, cut]], axis=1), weights)
        parts.append(both[:, :LANES] + both[:, LANES:])
    return jnp.concatenate(parts, axis=1)


def own_slots(shape):
    row = lax.broadcasted_iota(jnp.int32, shape, 0) // HALF
    lane = lax.broadcasted_iota(jnp.int32, shape, 1) // 16
    return lane == row


def lane_in_block(shape):
    return (lax.broadcasted_iota(jnp.int32, shape, 1) % BLOCK).astype(F32)


def grad_kernel(xt_ref, g_ref, mom_ref, off_ref, rowf_ref, rowi_ref, lanef_ref, lanei_ref, exp_ref, comp_ref, new_ref, val_ref, moved_ref):
    moved_ref[...] = dot(xt_ref[...], g_ref[...]) + DECAY * mom_ref[...].astype(F32)
    off = jnp.concatenate([off_ref[0]] * FIVE, axis=0)
    slots = own_slots((FIVE * HALF, LANES))
    off = jnp.where(slots, off, 0.0).astype(BF)
    offsets = dot(off, exp_ref[...])
    odd = offsets >= BLOCK
    picked_rows = []
    for p in range(FIVE):
        high, low = split(moved_ref[p * BLOCK:(p + 1) * BLOCK, :])
        freq = dot(rowf_ref[...], jnp.concatenate([high, low, high], axis=0))
        cut = slice(p * HALF, (p + 1) * HALF)
        picked_rows.append(jnp.where(odd[cut], freq[HALF:], freq[:HALF]))
    high, low = split(jnp.concatenate(picked_rows, axis=0))
    spectrum = lane_transform(high, low, lanef_ref[...])
    column = jnp.where(odd, offsets - BLOCK, offsets)
    picked = jnp.where(column == lane_in_block(offsets.shape), spectrum, 0.0)
    high, low = split(picked)
    values = dot(high, comp_ref[...]) + dot(low, comp_ref[...])
    values = jnp.where(slots, values, 0.0)
    val_ref[0] = sum(values[p * HALF:(p + 1) * HALF] for p in range(FIVE))
    spread = lane_transform(high, low, lanei_ref[...])
    for p in range(FIVE):
        cut = slice(p * HALF, (p + 1) * HALF)
        part = spread[cut]
        high, low = split(jnp.concatenate([jnp.where(odd[cut], 0.0, part), jnp.where(odd[cut], part, 0.0)], axis=0))
        taken = dot(rowi_ref[...], jnp.concatenate([high, low, high], axis=0))
        rows = slice(p * BLOCK, (p + 1) * BLOCK)
        new_ref[rows, :] = (moved_ref[rows, :] - taken).astype(BF)


def update_kernel(val_ref, off_ref, rowi_ref, lanei_ref, exp_ref, exp2_ref, same_ref, up_ref, even_ref, odd_ref):
    groups = val_ref.shape[0]
    slots = own_slots((FIVE * HALF, LANES))
    even_ref[...] = jnp.zeros_like(even_ref)
    odd_ref[...] = jnp.zeros_like(odd_ref)
    lane = lane_in_block(even_ref.shape)

    def add_group(r, carry):
        off = jnp.concatenate([off_ref[r, 0]] * FIVE, axis=0)
        off = jnp.where(slots, off, 0.0).astype(BF)
        offsets = dot(off, exp_ref[...])
        val = jnp.where(slots, jnp.concatenate([val_ref[r, 0]] * FIVE, axis=0), 0.0)
        high, low = split(val)
        values = dot(jnp.concatenate([high, low], axis=1), exp2_ref[...])
        even_ref[...] += jnp.where(offsets == lane, values, 0.0)
        odd_ref[...] += jnp.where(offsets == lane + BLOCK, values, 0.0)
        return carry

    lax.fori_loop(0, groups, add_group, 0)
    even, odd = even_ref[...], odd_ref[...]
    squares = even * even + odd * odd
    high, low = split(even)
    spread_even = lane_transform(high, low, lanei_ref[...])
    high, low = split(odd)
    spread_odd = lane_transform(high, low, lanei_ref[...])
    for p in range(FIVE):
        cut = slice(p * HALF, (p + 1) * HALF)
        high, low = split(jnp.concatenate([spread_even[cut], spread_odd[cut]], axis=0))
        field = dot(rowi_ref[...], jnp.concatenate([high, low, high], axis=0))
        total = jnp.broadcast_to(jnp.sum(squares[cut], axis=0, keepdims=True), (8, squares.shape[1]))
        scales = []
        for q in range(squares.shape[1] // LANES):
            high, low = split(total[:, q * LANES:(q + 1) * LANES])
            scales.append(dot(high, same_ref[...]) + dot(low, same_ref[...]))
        power = jnp.concatenate(scales, axis=1)[:1]
        scale = lax.rsqrt(power * (1.0 / (BLOCK * BLOCK)) + EPSILON)
        up_ref[p * BLOCK:(p + 1) * BLOCK, :] = (field * scale).astype(BF)


def whole(shape):
    return pl.BlockSpec(shape, lambda i: (0,) * len(shape))


def grad_call(xt, g, mom, off, t):
    features, width = mom.shape
    chunks = features // CHUNK
    return pl.pallas_call(
        grad_kernel,
        grid=(chunks,),
        in_specs=[
            pl.BlockSpec((CHUNK, ROWS), lambda i: (i, 0)),
            whole(g.shape),
            pl.BlockSpec((CHUNK, width), lambda i: (i, 0)),
            pl.BlockSpec((1, HALF, LANES), lambda i: (i, 0, 0)),
        ] + [whole(t[n].shape) for n in ("row_fwd", "row_inv", "lane_fwd", "lane_inv", "expand", "compress")],
        out_specs=[
            pl.BlockSpec((CHUNK, width), lambda i: (i, 0)),
            pl.BlockSpec((1, HALF, LANES), lambda i: (i, 0, 0)),
        ],
        out_shape=[
            jax.ShapeDtypeStruct((features, width), BF),
            jax.ShapeDtypeStruct((chunks, HALF, LANES), F32),
        ],
        scratch_shapes=[pltpu.VMEM((CHUNK, width), F32)],
        compiler_params=pltpu.CompilerParams(vmem_limit_bytes=50 * 2**20),
    )(xt, g, mom, off, *(t[n] for n in ("row_fwd", "row_inv", "lane_fwd", "lane_inv", "expand", "compress")))


def update_call(values, off, t, width):
    groups, chunks = values.shape[:2]
    names = ("row_inv", "lane_inv", "expand", "expand2", "same")
    return pl.pallas_call(
        update_kernel,
        grid=(chunks,),
        in_specs=[
            pl.BlockSpec((groups, 1, HALF, LANES), lambda i: (0, i, 0, 0)),
            pl.BlockSpec((groups, 1, HALF, LANES), lambda i: (0, i, 0, 0)),
        ] + [whole(t[n].shape) for n in names],
        out_specs=pl.BlockSpec((CHUNK, width), lambda i: (i, 0)),
        out_shape=jax.ShapeDtypeStruct((chunks * CHUNK, width), BF),
        scratch_shapes=[pltpu.VMEM((FIVE * HALF, width), F32), pltpu.VMEM((FIVE * HALF, width), F32)],
        compiler_params=pltpu.CompilerParams(vmem_limit_bytes=50 * 2**20),
    )(values, off, *(t[n] for n in names))


def slot_offsets(picks):
    groups, block_rows, block_cols, count = picks.shape
    off = (picks % LANES).astype(F32)
    off = jnp.pad(off, ((0, 0), (0, 0), (0, 16 - block_cols), (0, 0)))
    off = off.reshape(groups, block_rows // FIVE, FIVE * 16, count)
    off = jnp.transpose(off, (0, 1, 3, 2))
    return jnp.pad(off, ((0, 0), (0, 0), (0, 0), (0, LANES - FIVE * 16)))


def body(tokens, output_grads, momentum, component_picks):
    width = momentum.shape[2]
    t = {name: jnp.asarray(table) for name, table in tables(width).items()}
    xt = lax.all_gather((tokens * BF(1.0 / math.sqrt(ROWS))).T, "tp", axis=0, tiled=True)
    off = slot_offsets(component_picks)
    own = lax.dynamic_index_in_dim(off, lax.axis_index("rep"), 0, keepdims=False)
    new_momentum, values = grad_call(xt, output_grads, momentum[0], own, t)
    gathered = lax.all_gather(values, "rep", axis=0)
    update = update_call(gathered, off, t, width)
    return (new_momentum[None], update)


def solution(mesh):
    return jax.shard_map(
        body,
        mesh=mesh,
        in_specs=(P("rep", "tp"), P("rep", "tp"), P("rep", None, "tp"), P(None, None, "tp", None)),
        out_specs=(P("rep", None, "tp"), P(None, "tp")),
        check_vma=False,
    )
```

time: 561 us -> 164 us (0.29)
  local copies, waits for them, and re-layouts: 225 us -> 10.8 us
  matrix products: 212 us -> 0 us
  waiting for transfers between devices: 0.68 us -> 76.5 us
  blocking collectives: 57.2 us -> 0 us
  Pallas kernels: 0 us -> 56.3 us
  other arithmetic: 45.3 us -> 5.17 us
    dot_general x7 -> x0, matrix products: 212 us -> none  [the longest x2 68.2 us: backward_blocks(): result = jnp.einsum('pibc,cj->pibj', halfway, cosine, precision=PRECISE)]
    and x18 -> x0, local copies, waits for them, and re-layouts: 104 us -> none  [slot_mask(): return (half_iota == half_row) & (col_iota == column)]
    all_gather x1 -> x2, waiting for transfers between devices: 0.01 us -> 76.4 us  [the longest x1 43.8 us: body(): gathered = lax.all_gather(values, 'rep', axis=0)]
    unnamed x34 -> x21, local copies, waits for them, and re-layouts: 79.8 us -> 3.69 us
    all_gather x1 -> x0, blocking collectives: 57.2 us -> none  [body(): gathered = lax.all_gather(values[None], 'rep', axis=0, tiled=True)]
    pallas_call x0 -> x2, Pallas kernels: none -> 56.3 us  [the longest x1 36.2 us: update_call(): pl.pallas_call(update_kernel, grid=(chunks,), in_specs=[pl.BlockSpec((gro...]
    eq x10 -> x0, other arithmetic: 34.9 us -> none  [slot_mask(): return (half_iota == half_row) & (col_iota == column)]
    eq x20 -> x0, local copies, waits for them, and re-layouts: 16.3 us -> none  [slot_mask(): return (half_iota == half_row) & (col_iota == column)]
  transfers between devices with their start and end apart: 1 -> 2, of which waited for: 0 -> 2; matrix products, arithmetic and copies ran while one was open for 29% -> 8% of each run, Pallas kernels for 0% -> 0%
where the time goes in v1:
time: 164 us; the launch traced here: 163 us
  waiting for transfers between devices  76.5 us (47%)
  Pallas kernels  56.3 us (34%)
  between operations  14.1 us (9%)
  local copies, waits for them, and re-layouts  10.8 us (7%)
  other arithmetic  5.17 us (3%)
    all_gather x1, waiting for transfers between devices, body(): gathered = lax.all_gather(values, 'rep', axis=0)  43.8 us
    pallas_call x1, Pallas kernels, update_call(): pl.pallas_call(update_kernel, grid=(chunks,), in_specs=[pl.BlockSpec((gro...  36.2 us
    all_gather x1, waiting for transfers between devices, body(): lax.all_gather((tokens * BF(1.0 / math.sqrt(ROWS))).T, 'tp', axis=0, tile...  32.6 us
    pallas_call x1, Pallas kernels, grad_call(): pl.pallas_call(grad_kernel, grid=(chunks,), in_specs=[pl.BlockSpec((CHUNK...  20.2 us
    unnamed x21, local copies, waits for them, and re-layouts  3.69 us
    convert_element_type x1, other arithmetic, slot_offsets(): off = (picks % LANES).astype(F32)  3.44 us
  transfers between devices with their start and end apart: 2, of which 2 were waited for; matrix products, arithmetic and copies ran while one was open for 8% of the time, Pallas kernels for 0%

profile of v1, /device:TPU:1, one launch (start us, length us, event | category | flops | bytes accessed | tf_op | source)
XLA Modules:
  0.0 163.0 jit_solution(897012422233222705)
XLA Ops:
  7.2 0.0 all-gather.4.cloned.1.call-start
  7.2 1.7 %multiply_bitcast_fusion = bf16[160,1024]{1,0:T(8,128)(2,1)} fusion(bf16[1024,160]{0,1:T(8,128)(2,1)} %param.12), kind=kLoop, calls=%fused_computation.5 | loop fusion | flops 163840 | bytes 655360 | tf_op jit(solution)/shard_map/transpose | solution.py:224
  8.9 0.0 all-gather.4.cloned.1.call-update
  9.0 0.0 all-gather.6.cloned.1.call-start
  9.0 3.4 %fusion.1 = f32[8,40,14,32]{1,3,2,0:T(8,128)} fusion(s32[8,40,14,32]{1,3,2,0:T(8,128)} %param.15), kind=kLoop, calls=%fused_computation.4 | loop fusion | flops 1720320 | bytes 1146880 | tf_op jit(solution)/shard_map/convert_element_type | solution.py:214
  12.5 2.4 %copy.18 = f32[8,40,14,32]{3,2,1,0:T(8,128)S(1)} copy(f32[8,40,14,32]{1,3,2,0:T(8,128)} %fusion.1) | data formatting | bytes 1146880
  14.9 1.7 %pad.8.clone = f32[8,40,16,32]{3,2,1,0:T(8,128)} pad(f32[8,40,14,32]{3,2,1,0:T(8,128)S(1)} %copy.18, f32[]{:T(128)} %constant.43.clone.1), padding=0_0x0_0x0_2x0_0 | pad | bytes 1228804 | tf_op jit(solution)/shard_map/jit(_pad)/pad | solution.py:215
  16.6 0.0 copy-start.6
  16.7 0.0 copy-start.7
  16.7 0.0 copy-start.8
  16.7 3.1 %copy.17 = f32[8,8,80,32]{2,3,1,0:T(8,128)} copy(f32[8,8,80,32]{3,2,1,0:T(8,128)} %bitcast.10) | data formatting | bytes 1310720 | tf_op jit(solution)/shard_map/reshape | solution.py:216
  19.8 0.9 dynamic-slice_bitcast_fusion.off_ref
  20.7 32.6 %all-gather.4.cloned.1.call-done.xt_ref = bf16[2560,1024]{1,0:T(8,128)(2,1)} async-done(((bf16[160,1024]{1,0:T(8,128)(2,1)}), bf16[2560,1024]{1,0:T(8,128)(2,1)}) %all-gather.4.cloned.1.call-update) | async-done | bytes 5242896 | tf_op jit(solution)/shard_map/all_gather | solution.py:224
  53.3 0.0 copy-done
  53.3 0.0 copy-done.2
  53.3 0.0 copy-done.3
  53.3 0.0 copy-done.5
  53.3 20.2 %shard_map.131 = (bf16[2560,896]{1,0:T(8,128)(2,1)}, f32[8,32,128]{2,1,0:T(8,128)}) custom-call(bf16[2560,1024]{1,0:T(8,128)(2,1)} %all-gather.4.cloned.1.call-done.xt_ref, bf16[1024,896]{1,0:T(8,128)(2,1)S(1)} %copy-done, bf16[2560,896]{1,0:T(8,128)(2,1)} %bitcast.13, f32[8,32,128]{2,1,0:T(8,128)S(1)} %dynamic-slice_bitcast_fusion.off_ref, ...), custom_call_target="tpu_custom_call" | custom-call | tf_op jit(solution)/shard_map/pallas_call | solution.py:173
  73.5 0.0 all-gather.6.cloned.1.call-update
  73.5 1.4 pad.9.off_ref
  74.9 43.8 %all-gather.6.cloned.1.call-done = f32[64,32,128]{2,1,0:T(8,128)} async-done(((f32[8,32,128]{2,1,0:T(8,128)}), f32[64,32,128]{2,1,0:T(8,128)}) %all-gather.6.cloned.1.call-update) | async-done | bytes 1048592 | tf_op jit(solution)/shard_map/all_gather | solution.py:228
  118.7 0.0 copy-done.4
  118.8 1.2 copy-done.1
  120.0 36.2 %shard_map.132 = bf16[2560,896]{1,0:T(8,128)(2,1)} custom-call(f32[8,8,32,128]{3,2,1,0:T(8,128)S(1)} %bitcast.9, f32[8,8,32,128]{3,2,1,0:T(8,128)S(1)} %pad.9.off_ref, bf16[64,192]{1,0:T(8,128)(2,1)S(1)} %copy-done.7, bf16[256,256]{1,0:T(8,128)(2,1)S(1)} %copy-done.3, bf16[128,896]{1,0:T(8,128)(2,1)S(1)} %copy-done.2, bf16[256,896]{1,0:T(8,128)(2,1)S(1)} %copy-done.4, ...), custom_call_target="tpu_custom_call" | custom-call | tf_op jit(solution)/shard_map/pallas_call | solution.py:198
  (11 shorter events, 0.0 us)
Async XLA Ops:
  7.2 46.1 %all-gather.4.cloned.1.call-start = ((), (), s32[]{:S(2)}) async-start(), calls=%async_computation | async-start | bytes 5570560 | tf_op jit(solution)/shard_map/all_gather | solution.py:224
  9.0 109.8 %all-gather.6.cloned.1.call-start = ((), (), s32[]{:S(2)}) async-start(), calls=%async_computation.1 | async-start | bytes 1179648 | tf_op jit(solution)/shard_map/all_gather | solution.py:228
  16.6 36.6 %copy-start = (bf16[1024,896]{1,0:T(8,128)(2,1)S(1)}, bf16[1024,896]{1,0:T(8,128)(2,1)}, u32[]{:S(2)}) copy-start(bf16[1024,896]{1,0:T(8,128)(2,1)} %g_ref.1) | copy-start | bytes 5505028
  16.6 36.6 %copy-start.2 = (bf16[128,896]{1,0:T(8,128)(2,1)S(1)}, bf16[128,896]{1,0:T(8,128)(2,1)}, u32[]{:S(2)}) copy-start(bf16[128,896]{1,0:T(8,128)(2,1)} %constant.51.clone.exp_ref) | copy-start | bytes 688132
  16.6 36.6 %copy-start.3 = (bf16[256,256]{1,0:T(8,128)(2,1)S(1)}, bf16[256,256]{1,0:T(8,128)(2,1)}, u32[]{:S(2)}) copy-start(bf16[256,256]{1,0:T(8,128)(2,1)} %constant.50.clone.lanei_ref) | copy-start | bytes 393220
  16.6 36.6 %copy-start.5 = (bf16[896,128]{1,0:T(8,128)(2,1)S(1)}, bf16[896,128]{1,0:T(8,128)(2,1)}, u32[]{:S(2)}) copy-start(bf16[896,128]{1,0:T(8,128)(2,1)} %constant.53.clone.comp_ref) | copy-start | bytes 688132
  16.6 36.6 %copy-start.6 = (bf16[256,256]{1,0:T(8,128)(2,1)S(1)}, bf16[256,256]{1,0:T(8,128)(2,1)}, u32[]{:S(2)}) copy-start(bf16[256,256]{1,0:T(8,128)(2,1)} %constant.49.clone.lanef_ref) | copy-start | bytes 393220
  16.7 36.6 %copy-start.7 = (bf16[64,192]{1,0:T(8,128)(2,1)S(1)}, bf16[64,192]{1,0:T(8,128)(2,1)}, u32[]{:S(2)}) copy-start(bf16[64,192]{1,0:T(8,128)(2,1)} %constant.48.clone.rowi_ref) | copy-start | bytes 73732
  16.7 36.6 %copy-start.8 = (bf16[64,192]{1,0:T(8,128)(2,1)S(1)}, bf16[64,192]{1,0:T(8,128)(2,1)}, u32[]{:S(2)}) copy-start(bf16[64,192]{1,0:T(8,128)(2,1)} %constant.47.clone.rowf_ref) | copy-start | bytes 73732
  73.5 45.3 %copy-start.4 = (bf16[256,896]{1,0:T(8,128)(2,1)S(1)}, bf16[256,896]{1,0:T(8,128)(2,1)}, u32[]{:S(2)}) copy-start(bf16[256,896]{1,0:T(8,128)(2,1)} %constant.52.clone.exp2_ref) | copy-start | bytes 1376260
  73.5 45.3 %copy-start.9 = (bf16[128,128]{1,0:T(8,128)(2,1)S(1)}, bf16[128,128]{1,0:T(8,128)(2,1)}, u32[]{:S(2)}) copy-start(bf16[128,128]{1,0:T(8,128)(2,1)} %constant.54.clone.same_ref) | copy-start | bytes 98308
  118.7 1.2 copy-start.1
Sparse Core Ops, SparseCore 0:
  10.3 42.9 all-gather.3
  73.6 45.0 all-gather.5

commit v2 on v1

--- a/solution.py
+++ b/solution.py
@@ -93,9 +93,204 @@
     return (lax.broadcasted_iota(jnp.int32, shape, 1) % BLOCK).astype(F32)
 
 
-def grad_kernel(xt_ref, g_ref, mom_ref, off_ref, rowf_ref, rowi_ref, lanef_ref, lanei_ref, exp_ref, comp_ref, new_ref, val_ref, moved_ref):
-    moved_ref[...] = dot(xt_ref[...], g_ref[...]) + DECAY * mom_ref[...].astype(F32)
-    off = jnp.concatenate([off_ref[0]] * FIVE, axis=0)
+def gather_kernel(xt_ref, g_hbm, mom_hbm, picks_ref, rowf_ref, rowi_ref, lanef_ref, lanei_ref, exp_ref, comp_ref,
+                  new_hbm, val_hbm, off_hbm,
+                  xt, g, mom, new, moved, turned, off_all, val_all,
+                  g_sem, mom_sem, new_sem, out_sem, own_sem, send_sem, recv_sem, pass_sem, sib_sem, vsend_sem, vrecv_sem):
+    share = xt_ref.shape[0]
+    chips = mom.shape[0] // CHUNK
+    line = chips // 2
+    reps = val_all.shape[0]
+    rep, tp = lax.axis_index("rep"), lax.axis_index("tp")
+    core, chip = lax.rem(tp, 2), lax.div(tp, 2)
+    x, y = lax.rem(chip, line), lax.div(chip, line)
+
+    def chip_at(dx, dy):
+        return lax.rem(y + dy, 2) * line + lax.rem(x + dx, line)
+
+    def device_at(dx, dy):
+        return {"tp": chip_at(dx, dy) * 2 + core}
+
+    left, right, across, sibling = device_at(line - 1, 0), device_at(1, 0), device_at(0, 1), {"tp": chip * 2 + 1 - core}
+
+    def chip_of(step):
+        dy = jnp.where((step == 3) | (step >= 5), 1, 0)
+        dx = jnp.where((step == 1) | (step == 5), line - 1, jnp.where((step == 2) | (step == 6), 1, jnp.where((step == 4) | (step == 7), 2, 0)))
+        return chip_at(dx, dy)
+
+    def rows_of(step, first, count):
+        start = (chip_of(step) * 2 + core) * share + first
+        return xt.at[pl.ds(pl.multiple_of(start, 16), count), :]
+
+    half = share // 2
+
+    def push(index, recv, step, first, count, target, source=None):
+        rows = rows_of(step, first, count)
+        return pltpu.make_async_remote_copy(
+            src_ref=rows if source is None else source, dst_ref=rows,
+            send_sem=send_sem.at[index], recv_sem=recv_sem.at[recv],
+            device_id=target, device_id_type=pl.DeviceIdType.MESH)
+
+    def arrive(recv, step, first, count):
+        push(0, recv, step, first, count, left).wait_recv()
+
+    def to_sibling(step, source=None):
+        rows = rows_of(step, 0, share)
+        return pltpu.make_async_remote_copy(
+            src_ref=rows if source is None else source, dst_ref=rows,
+            send_sem=pass_sem.at[step], recv_sem=sib_sem.at[step],
+            device_id=sibling, device_id_type=pl.DeviceIdType.MESH)
+
+    def from_sibling(step):
+        start = (chip_of(step) * 2 + 1 - core) * share
+        rows = xt.at[pl.ds(pl.multiple_of(start, 16), share), :]
+        pltpu.make_async_remote_copy(
+            src_ref=rows, dst_ref=rows, send_sem=pass_sem.at[step], recv_sem=sib_sem.at[step],
+            device_id=sibling, device_id_type=pl.DeviceIdType.MESH).wait_recv()
+
+    def mom_copy(step):
+        rows = pl.ds(pl.multiple_of(chip_of(step) * CHUNK, CHUNK), CHUNK)
+        return pltpu.make_async_copy(mom_hbm.at[rows, :], mom.at[rows, :], mom_sem.at[step])
+
+    def new_copy(step):
+        rows = pl.ds(pl.multiple_of(chip_of(step) * CHUNK, CHUNK), CHUNK)
+        return pltpu.make_async_copy(new.at[rows, :], new_hbm.at[rows, :], new_sem.at[step])
+
+    def send_values(part, first, count, ahead):
+        slab = val_all.at[rep, pl.ds(first, count)]
+        return pltpu.make_async_remote_copy(
+            src_ref=slab, dst_ref=slab,
+            send_sem=vsend_sem.at[part, ahead], recv_sem=vrecv_sem.at[part, ahead],
+            device_id={"rep": lax.rem(rep + ahead, reps)}, device_id_type=pl.DeviceIdType.MESH)
+
+    def take_values(part, first, count, behind):
+        slab = val_all.at[lax.rem(rep + reps - behind, reps), pl.ds(first, count)]
+        return pltpu.make_async_remote_copy(
+            src_ref=slab, dst_ref=slab,
+            send_sem=vsend_sem.at[part, behind], recv_sem=vrecv_sem.at[part, behind],
+            device_id={"rep": lax.rem(rep + behind, reps)}, device_id_type=pl.DeviceIdType.MESH)
+
+    g_copy = pltpu.make_async_copy(g_hbm, g, g_sem)
+    g_copy.start()
+    own_rows = rows_of(0, 0, share)
+    own_copy = pltpu.make_async_copy(xt_ref, own_rows, own_sem)
+    own_copy.start()
+    mom_copy(0).start()
+
+    barrier = pltpu.get_barrier_semaphore()
+    for target in (left, right, across, sibling):
+        pl.semaphore_signal(barrier, inc=1, device_id=target, device_id_type=pl.DeviceIdType.MESH)
+    for ahead in range(1, reps):
+        pl.semaphore_signal(barrier, inc=1, device_id={"rep": lax.rem(rep + ahead, reps)}, device_id_type=pl.DeviceIdType.MESH)
+    pl.semaphore_wait(barrier, 4 + reps - 1)
+
+    first_pushes = [push(0, 0, 0, 0, share, right, xt_ref), push(1, 1, 0, 0, share, left, xt_ref), push(2, 2, 0, 0, share, across, xt_ref)]
+    to_sibling(0, xt_ref).start()
+    for copy in first_pushes:
+        copy.start()
+    for step in range(1, chips):
+        mom_copy(step).start()
+
+    turned[...] = jnp.zeros_like(turned)
+
+    def turn(index, carry):
+        part, quad = lax.div(index, 2), lax.rem(index, 2)
+        for p in range(FIVE):
+            for r in range(4):
+                picks = picks_ref[quad * 4 + r, part * FIVE + p]
+                turned[p * 16:p * 16 + picks.shape[0], r * HALF:(r + 1) * HALF] = (picks & (LANES - 1)).astype(F32)
+        flat = turned[...].T
+        for r in range(4):
+            off_all[quad * 4 + r, part] = flat[r * HALF:(r + 1) * HALF]
+        return carry
+
+    lax.fori_loop(0, chips * 2, turn, 0)
+    off_copy = pltpu.make_async_copy(off_all, off_hbm, out_sem.at[0])
+    off_copy.start()
+    own_copy.wait()
+    g_copy.wait()
+
+    second_pushes = [
+        push(3, 3, 1, 0, half, right), push(4, 4, 2, half, half, left),
+        push(5, 5, 3, 0, share, right), push(6, 6, 3, 0, share, left)]
+    third_pushes = [push(7, 7, 4, 0, half, across), push(8, 8, 4, half, half, across)]
+
+    def one(step, carry):
+        @pl.when(step == 1)
+        def _():
+            arrive(0, 1, 0, share)
+            arrive(1, 2, 0, share)
+            arrive(2, 3, 0, share)
+            for copy in second_pushes:
+                copy.start()
+            for s in (1, 2, 3):
+                to_sibling(s).start()
+
+        @pl.when(step == 2)
+        def _():
+            arrive(3, 4, 0, half)
+            arrive(4, 4, half, half)
+            for copy in third_pushes:
+                copy.start()
+            to_sibling(4).start()
+
+        @pl.when(step == 5)
+        def _():
+            arrive(5, 5, 0, share)
+            to_sibling(5).start()
+            arrive(6, 6, 0, share)
+            to_sibling(6).start()
+            arrive(7, 7, 0, half)
+            arrive(8, 7, half, half)
+            to_sibling(7).start()
+
+        from_sibling(step)
+        mom_copy(step).wait()
+        chunk = chip_of(step)
+        base = pl.multiple_of(chunk * CHUNK, CHUNK)
+        values = grad_chunk(xt, g, mom, off_all[rep, chunk], rowf_ref, rowi_ref, lanef_ref, lanei_ref, exp_ref, comp_ref, new, moved, base)
+        val_all[rep, step] = values
+        new_copy(step).start()
+
+        @pl.when(step == 3)
+        def _():
+            for ahead in range(1, reps):
+                send_values(0, 0, 4, ahead).start()
+
+        @pl.when(step == 6)
+        def _():
+            for ahead in range(1, reps):
+                send_values(1, 4, 3, ahead).start()
+
+        return carry
+
+    lax.fori_loop(0, chips, one, 0)
+    for ahead in range(1, reps):
+        send_values(2, 7, 1, ahead).start()
+    for copy in first_pushes + second_pushes + third_pushes:
+        copy.wait_send()
+    for step in range(chips):
+        to_sibling(step).wait_send()
+        new_copy(step).wait()
+    off_copy.wait()
+    parts = ((0, 0, 4), (1, 4, 3), (2, 7, 1))
+    for part, first, count in parts:
+        for behind in range(1, reps):
+            take_values(part, first, count, behind).wait_recv()
+    outs = [pltpu.make_async_copy(val_all.at[:, step], val_hbm.at[:, chip_of(step)], out_sem.at[1 + step]) for step in range(chips)]
+    for copy in outs:
+        copy.start()
+    for part, first, count in parts:
+        for ahead in range(1, reps):
+            send_values(part, first, count, ahead).wait_send()
+    for copy in outs:
+        copy.wait()
+
+
+def grad_chunk(xt, g, mom, off, rowf_ref, rowi_ref, lanef_ref, lanei_ref, exp_ref, comp_ref, new, moved_ref, base):
+    rows = pl.ds(base, CHUNK)
+    moved_ref[...] = dot(xt[rows, :], g[...]) + DECAY * mom[rows, :].astype(F32)
+    off = jnp.concatenate([off] * FIVE, axis=0)
     slots = own_slots((FIVE * HALF, LANES))
     off = jnp.where(slots, off, 0.0).astype(BF)
     offsets = dot(off, exp_ref[...])
@@ -113,18 +308,23 @@
     high, low = split(picked)
     values = dot(high, comp_ref[...]) + dot(low, comp_ref[...])
     values = jnp.where(slots, values, 0.0)
-    val_ref[0] = sum(values[p * HALF:(p + 1) * HALF] for p in range(FIVE))
     spread = lane_transform(high, low, lanei_ref[...])
     for p in range(FIVE):
         cut = slice(p * HALF, (p + 1) * HALF)
         part = spread[cut]
         high, low = split(jnp.concatenate([jnp.where(odd[cut], 0.0, part), jnp.where(odd[cut], part, 0.0)], axis=0))
         taken = dot(rowi_ref[...], jnp.concatenate([high, low, high], axis=0))
-        rows = slice(p * BLOCK, (p + 1) * BLOCK)
-        new_ref[rows, :] = (moved_ref[rows, :] - taken).astype(BF)
-
-
-def update_kernel(val_ref, off_ref, rowi_ref, lanei_ref, exp_ref, exp2_ref, same_ref, up_ref, even_ref, odd_ref):
+        new[pl.ds(base + p * BLOCK, BLOCK), :] = (moved_ref[p * BLOCK:(p + 1) * BLOCK, :] - taken).astype(BF)
+    return sum(values[p * HALF:(p + 1) * HALF] for p in range(FIVE))
+
+
+def update_kernel(val_ref, off_ref, rowi_ref, lanei_ref, exp_ref, exp2_ref, same_ref, new_in, up_ref, new_out, even_ref, odd_ref, sem):
+    keep = pltpu.make_async_copy(new_in, new_out, sem)
+
+    @pl.when(pl.program_id(0) == 0)
+    def _():
+        keep.start()
+
     groups = val_ref.shape[0]
     slots = own_slots((FIVE * HALF, LANES))
     even_ref[...] = jnp.zeros_like(even_ref)
@@ -162,37 +362,47 @@
         scale = lax.rsqrt(power * (1.0 / (BLOCK * BLOCK)) + EPSILON)
         up_ref[p * BLOCK:(p + 1) * BLOCK, :] = (field * scale).astype(BF)
 
+    @pl.when(pl.program_id(0) == pl.num_programs(0) - 1)
+    def _():
+        keep.wait()
+
 
 def whole(shape):
     return pl.BlockSpec(shape, lambda i: (0,) * len(shape))
 
 
-def grad_call(xt, g, mom, off, t):
+def gather_call(xt, g, mom, picks, t):
     features, width = mom.shape
+    reps = picks.shape[0]
     chunks = features // CHUNK
+    names = ("row_fwd", "row_inv", "lane_fwd", "lane_inv", "expand", "compress")
+    vmem, any_space = pl.BlockSpec(memory_space=pltpu.VMEM), pl.BlockSpec(memory_space=pl.ANY)
+    dma = pltpu.SemaphoreType.DMA
     return pl.pallas_call(
-        grad_kernel,
-        grid=(chunks,),
-        in_specs=[
-            pl.BlockSpec((CHUNK, ROWS), lambda i: (i, 0)),
-            whole(g.shape),
-            pl.BlockSpec((CHUNK, width), lambda i: (i, 0)),
-            pl.BlockSpec((1, HALF, LANES), lambda i: (i, 0, 0)),
-        ] + [whole(t[n].shape) for n in ("row_fwd", "row_inv", "lane_fwd", "lane_inv", "expand", "compress")],
-        out_specs=[
-            pl.BlockSpec((CHUNK, width), lambda i: (i, 0)),
-            pl.BlockSpec((1, HALF, LANES), lambda i: (i, 0, 0)),
-        ],
+        gather_kernel,
+        in_specs=[any_space, any_space, any_space] + [vmem] * (1 + len(names)),
+        out_specs=[any_space] * 3,
         out_shape=[
             jax.ShapeDtypeStruct((features, width), BF),
-            jax.ShapeDtypeStruct((chunks, HALF, LANES), F32),
+            jax.ShapeDtypeStruct((reps, chunks, HALF, LANES), F32),
+            jax.ShapeDtypeStruct((reps, chunks, HALF, LANES), F32),
         ],
-        scratch_shapes=[pltpu.VMEM((CHUNK, width), F32)],
-        compiler_params=pltpu.CompilerParams(vmem_limit_bytes=50 * 2**20),
-    )(xt, g, mom, off, *(t[n] for n in ("row_fwd", "row_inv", "lane_fwd", "lane_inv", "expand", "compress")))
-
-
-def update_call(values, off, t, width):
+        scratch_shapes=[
+            pltpu.VMEM((features, ROWS), BF),
+            pltpu.VMEM(g.shape, BF),
+            pltpu.VMEM((features, width), BF),
+            pltpu.VMEM((features, width), BF),
+            pltpu.VMEM((CHUNK, width), F32),
+            pltpu.VMEM((LANES, LANES), F32),
+            pltpu.VMEM((reps, chunks, HALF, LANES), F32),
+            pltpu.VMEM((reps, chunks, HALF, LANES), F32),
+            dma, dma((chunks,)), dma((chunks,)), dma((1 + chunks,)), dma, dma((9,)), dma((9,)), dma((chunks,)), dma((chunks,)), dma((3, reps)), dma((3, reps)),
+        ],
+        compiler_params=pltpu.CompilerParams(vmem_limit_bytes=56 * 2**20, collective_id=0, has_side_effects=True),
+    )(xt, g, mom, picks, *(t[n] for n in names))
+
+
+def update_call(values, off, new, t, width):
     groups, chunks = values.shape[:2]
     names = ("row_inv", "lane_inv", "expand", "expand2", "same")
     return pl.pallas_call(
@@ -201,32 +411,20 @@
         in_specs=[
             pl.BlockSpec((groups, 1, HALF, LANES), lambda i: (0, i, 0, 0)),
             pl.BlockSpec((groups, 1, HALF, LANES), lambda i: (0, i, 0, 0)),
-        ] + [whole(t[n].shape) for n in names],
-        out_specs=pl.BlockSpec((CHUNK, width), lambda i: (i, 0)),
-        out_shape=jax.ShapeDtypeStruct((chunks * CHUNK, width), BF),
-        scratch_shapes=[pltpu.VMEM((FIVE * HALF, width), F32), pltpu.VMEM((FIVE * HALF, width), F32)],
+        ] + [whole(t[n].shape) for n in names] + [pl.BlockSpec(memory_space=pl.ANY)],
+        out_specs=[pl.BlockSpec((CHUNK, width), lambda i: (i, 0)), pl.BlockSpec(memory_space=pl.ANY)],
+        out_shape=[jax.ShapeDtypeStruct((chunks * CHUNK, width), BF), jax.ShapeDtypeStruct(new.shape, BF)],
+        scratch_shapes=[pltpu.VMEM((FIVE * HALF, width), F32), pltpu.VMEM((FIVE * HALF, width), F32), pltpu.SemaphoreType.DMA],
         compiler_params=pltpu.CompilerParams(vmem_limit_bytes=50 * 2**20),
-    )(values, off, *(t[n] for n in names))
-
-
-def slot_offsets(picks):
-    groups, block_rows, block_cols, count = picks.shape
-    off = (picks % LANES).astype(F32)
-    off = jnp.pad(off, ((0, 0), (0, 0), (0, 16 - block_cols), (0, 0)))
-    off = off.reshape(groups, block_rows // FIVE, FIVE * 16, count)
-    off = jnp.transpose(off, (0, 1, 3, 2))
-    return jnp.pad(off, ((0, 0), (0, 0), (0, 0), (0, LANES - FIVE * 16)))
+    )(values, off, *(t[n] for n in names), new)
 
 
 def body(tokens, output_grads, momentum, component_picks):
     width = momentum.shape[2]
     t = {name: jnp.asarray(table) for name, table in tables(width).items()}
-    xt = lax.all_gather((tokens * BF(1.0 / math.sqrt(ROWS))).T, "tp", axis=0, tiled=True)
-    off = slot_offsets(component_picks)
-    own = lax.dynamic_index_in_dim(off, lax.axis_index("rep"), 0, keepdims=False)
-    new_momentum, values = grad_call(xt, output_grads, momentum[0], own, t)
-    gathered = lax.all_gather(values, "rep", axis=0)
-    update = update_call(gathered, off, t, width)
+    xt = (tokens * BF(1.0 / math.sqrt(ROWS))).T
+    new_momentum, values, off = gather_call(xt, output_grads, momentum[0], component_picks, t)
+    update, new_momentum = update_call(values, off, new_momentum, t, width)
     return (new_momentum[None], update)
 
 

time: 164 us -> 198 us (1.21)
  Pallas kernels: 56.3 us -> 189 us
  waiting for transfers between devices: 76.5 us -> 0 us
  between operations: 14.1 us -> 0.7 us
  local copies, waits for them, and re-layouts: 10.8 us -> 5.73 us
  other arithmetic: 5.17 us -> 1.73 us
    pallas_call x1, Pallas kernels: 36.2 us -> 141 us  [update_call(): pl.pallas_call(update_kernel, grid=(chunks,), in_specs=[pl.BlockSpec((gro...]
    all_gather x2 -> x0, waiting for transfers between devices: 76.4 us -> none  [the longest x1 43.8 us: body(): gathered = lax.all_gather(values, 'rep', axis=0)]
    pallas_call x1, Pallas kernels: 20.2 us -> 48.5 us  [gather_call(): pl.pallas_call(gather_kernel, in_specs=[any_space, any_space, any_space]...]
    convert_element_type x1 -> x0, other arithmetic: 3.44 us -> none  [slot_offsets(): off = (picks % LANES).astype(F32)]
    pad x2 -> x0, local copies, waits for them, and re-layouts: 3.15 us -> none  [the longest x1 1.74 us: slot_offsets(): off = jnp.pad(off, ((0, 0), (0, 0), (0, 16 - block_cols), (0, 0)))]
    reshape x1 -> x0, local copies, waits for them, and re-layouts: 3.08 us -> none  [slot_offsets(): off = off.reshape(groups, block_rows // FIVE, FIVE * 16, count)]
    unnamed x21 -> x15, local copies, waits for them, and re-layouts: 3.69 us -> 5.73 us
  transfers between devices with their start and end apart: 2 -> 0, of which waited for: 2 -> 0; matrix products, arithmetic and copies ran while one was open for 8% -> 0% of each run, Pallas kernels for 0% -> 0%
where the time goes in v2:
time: 198 us
  Pallas kernels  189 us (95%)
  local copies, waits for them, and re-layouts  5.73 us (3%)
    pallas_call x1, Pallas kernels, update_call(): pl.pallas_call(update_kernel, grid=(chunks,), in_specs=[pl.BlockSpec((gro...  141 us
    pallas_call x1, Pallas kernels, gather_call(): pl.pallas_call(gather_kernel, in_specs=[any_space, any_space, any_space]...  48.5 us
    unnamed x15, local copies, waits for them, and re-layouts  5.73 us

profile of v2, /device:TPU:1, one launch (start us, length us, event | category | flops | bytes accessed | tf_op | source)
XLA Modules:
  0.0 197.6 jit_solution(7874068973509660357)
XLA Ops:
  0.6 1.7 multiply_bitcast_fusion.xt_ref
  2.4 3.3 %copy.14.picks_ref = s32[8,40,14,32]{3,2,1,0:T(8,128)} copy(s32[8,40,14,32]{1,3,2,0:T(8,128)} %param.15) | data formatting | bytes 1146880 | tf_op args[3]
  5.6 0.0 copy-start.2
  5.6 0.0 copy-start.3
  5.6 0.0 copy-start.4
  5.6 0.0 copy-start.5
  5.6 0.0 copy-start.6
  5.6 48.5 %shard_map.131 = (bf16[2560,896]{1,0:T(8,128)(2,1)}, f32[8,8,32,128]{3,2,1,0:T(8,128)}, f32[8,8,32,128]{3,2,1,0:T(8,128)}) custom-call(bf16[160,1024]{1,0:T(8,128)(2,1)} %multiply_bitcast_fusion.xt_ref, bf16[1024,896]{1,0:T(8,128)(2,1)} %g_hbm.1, bf16[2560,896]{1,0:T(8,128)(2,1)} %bitcast.4, s32[8,40,14,32]{3,2,1,0:T(8,128)} %copy.14.picks_ref, ...), custom_call_target="tpu_custom_call" | custom-call | tf_op jit(solution)/shard_map/pallas_call | solution.py:381
  54.1 0.0 copy-done.2
  54.1 0.0 copy-done.3
  54.1 0.0 copy-done.4
  54.2 0.0 copy-done.5
  54.2 0.0 copy-done.6
  54.2 0.0 copy-start
  54.2 1.2 copy-done
  55.4 0.0 copy-start.1
  55.4 1.2 copy-done.1
  56.6 141.0 %shard_map.132 = (bf16[2560,896]{1,0:T(8,128)(2,1)}, bf16[2560,896]{1,0:T(8,128)(2,1)}) custom-call(f32[8,8,32,128]{3,2,1,0:T(8,128)S(1)} %copy-done, f32[8,8,32,128]{3,2,1,0:T(8,128)S(1)} %copy-done.1, bf16[64,192]{1,0:T(8,128)(2,1)S(1)} %copy-done.5, bf16[256,256]{1,0:T(8,128)(2,1)S(1)} %copy-done.3, bf16[128,896]{1,0:T(8,128)(2,1)S(1)} %copy-done.2, ...), custom_call_target="tpu_custom_call" | custom-call | tf_op jit(solution)/shard_map/pallas_call | solution.py:408
Async XLA Ops:
  5.6 48.5 %copy-start.2 = (bf16[128,896]{1,0:T(8,128)(2,1)S(1)}, bf16[128,896]{1,0:T(8,128)(2,1)}, u32[]{:S(2)}) copy-start(bf16[128,896]{1,0:T(8,128)(2,1)} %constant.22.clone.exp_ref) | copy-start | bytes 688132
  5.6 48.5 %copy-start.3 = (bf16[256,256]{1,0:T(8,128)(2,1)S(1)}, bf16[256,256]{1,0:T(8,128)(2,1)}, u32[]{:S(2)}) copy-start(bf16[256,256]{1,0:T(8,128)(2,1)} %constant.21.clone.lanei_ref) | copy-start | bytes 393220
  5.6 48.5 %copy-start.4 = (bf16[256,896]{1,0:T(8,128)(2,1)S(1)}, bf16[256,896]{1,0:T(8,128)(2,1)}, u32[]{:S(2)}) copy-start(bf16[256,896]{1,0:T(8,128)(2,1)} %constant.23.clone.exp2_ref) | copy-start | bytes 1376260
  5.6 48.5 %copy-start.5 = (bf16[64,192]{1,0:T(8,128)(2,1)S(1)}, bf16[64,192]{1,0:T(8,128)(2,1)}, u32[]{:S(2)}) copy-start(bf16[64,192]{1,0:T(8,128)(2,1)} %constant.19.clone.rowi_ref) | copy-start | bytes 73732
  5.6 48.5 %copy-start.6 = (bf16[128,128]{1,0:T(8,128)(2,1)S(1)}, bf16[128,128]{1,0:T(8,128)(2,1)}, u32[]{:S(2)}) copy-start(bf16[128,128]{1,0:T(8,128)(2,1)} %constant.25.clone.same_ref) | copy-start | bytes 98308
  54.2 1.2 copy-start
  55.4 1.2 copy-start.1

commit v3 on v2

--- a/solution.py
+++ b/solution.py
@@ -16,8 +16,10 @@
 FIVE = 5
 CHUNK = FIVE * BLOCK
 LANES = 128
+SLOT = 8
 DECAY = 0.9
 EPSILON = 1e-06
+NAMES = ("select", "row_fwd", "row_inv", "lane_fwd", "lane_inv", "expand", "compress")
 BF = jnp.bfloat16
 F32 = jnp.float32
 
@@ -28,7 +30,7 @@
     return high, low
 
 
-def tables(width):
+def tables(width, width_rows):
     frequency = np.arange(BLOCK, dtype=np.float64)[:, None]
     position = np.arange(BLOCK, dtype=np.float64)[None, :]
     norm = np.where(frequency == 0, math.sqrt(1.0 / BLOCK), math.sqrt(2.0 / BLOCK))
@@ -48,11 +50,17 @@
             [np.concatenate([high, low], axis=1), np.concatenate([high, np.zeros_like(low)], axis=1)]
         )
 
-    slot = np.arange(LANES)[:, None] % 16
+    slot = np.arange(LANES)[:, None] // SLOT
     block = np.arange(width)[None, :] // BLOCK
     expand = (slot == block).astype(ml_dtypes.bfloat16)
     same = (np.arange(LANES)[:, None] // BLOCK == np.arange(LANES)[None, :] // BLOCK).astype(ml_dtypes.bfloat16)
+    rows = width_rows
+    select = np.zeros((width // BLOCK, rows, rows // FIVE * LANES), ml_dtypes.bfloat16)
+    for b in range(width // BLOCK):
+        for p in range(rows):
+            select[b, p, p // FIVE * LANES + b * SLOT + p % FIVE] = 1.0
     return {
+        "select": select,
         "row_fwd": rows_table(ordered),
         "row_inv": rows_table(ordered.T),
         "lane_fwd": lanes_table(cosine.T),
@@ -85,7 +93,7 @@
 
 def own_slots(shape):
     row = lax.broadcasted_iota(jnp.int32, shape, 0) // HALF
-    lane = lax.broadcasted_iota(jnp.int32, shape, 1) // 16
+    lane = lax.broadcasted_iota(jnp.int32, shape, 1) % SLOT
     return lane == row
 
 
@@ -93,10 +101,14 @@
     return (lax.broadcasted_iota(jnp.int32, shape, 1) % BLOCK).astype(F32)
 
 
-def gather_kernel(xt_ref, g_hbm, mom_hbm, picks_ref, rowf_ref, rowi_ref, lanef_ref, lanei_ref, exp_ref, comp_ref,
-                  new_hbm, val_hbm, off_hbm,
-                  xt, g, mom, new, moved, turned, off_all, val_all,
-                  g_sem, mom_sem, new_sem, out_sem, own_sem, send_sem, recv_sem, pass_sem, sib_sem, vsend_sem, vrecv_sem):
+def gather_kernel(xt_ref, g_hbm, mom_hbm, *refs):
+    count = len(NAMES) + 1
+    small_hbm, refs = refs[:count], refs[count:]
+    new_hbm, val_hbm, off_hbm = refs[:3]
+    small, refs = refs[3:3 + count], refs[3 + count:]
+    picks_ref, select_ref, rowf_ref, rowi_ref, lanef_ref, lanei_ref, exp_ref, comp_ref = small
+    (xt, g, mom, new, moved, off_all, val_all,
+                  small_sem, g_sem, mom_sem, new_sem, out_sem, own_sem, send_sem, recv_sem, pass_sem, sib_sem, vsend_sem, vrecv_sem) = refs
     share = xt_ref.shape[0]
     chips = mom.shape[0] // CHUNK
     line = chips // 2
@@ -170,11 +182,14 @@
             send_sem=vsend_sem.at[part, behind], recv_sem=vrecv_sem.at[part, behind],
             device_id={"rep": lax.rem(rep + behind, reps)}, device_id_type=pl.DeviceIdType.MESH)
 
-    g_copy = pltpu.make_async_copy(g_hbm, g, g_sem)
-    g_copy.start()
     own_rows = rows_of(0, 0, share)
     own_copy = pltpu.make_async_copy(xt_ref, own_rows, own_sem)
     own_copy.start()
+    small_copies = [pltpu.make_async_copy(small_hbm[n], small[n], small_sem.at[n]) for n in range(count)]
+    for copy in small_copies:
+        copy.start()
+    g_copy = pltpu.make_async_copy(g_hbm, g, g_sem)
+    g_copy.start()
     mom_copy(0).start()
 
     barrier = pltpu.get_barrier_semaphore()
@@ -182,6 +197,16 @@
         pl.semaphore_signal(barrier, inc=1, device_id=target, device_id_type=pl.DeviceIdType.MESH)
     for ahead in range(1, reps):
         pl.semaphore_signal(barrier, inc=1, device_id={"rep": lax.rem(rep + ahead, reps)}, device_id_type=pl.DeviceIdType.MESH)
+    small_copies[0].wait()
+    small_copies[1].wait()
+    flat = jnp.zeros((reps * HALF, chips * LANES), F32)
+    for b in range(picks_ref.shape[1]):
+        low_bits = (picks_ref[:, b] & (LANES - 1)).astype(F32).astype(BF)
+        flat = flat + dot(low_bits.reshape(reps * HALF, low_bits.shape[2]), select_ref[b])
+    for r in range(reps):
+        for part in range(chips):
+            off_all[r, part] = flat[r * HALF:(r + 1) * HALF, part * LANES:(part + 1) * LANES]
+
     pl.semaphore_wait(barrier, 4 + reps - 1)
 
     first_pushes = [push(0, 0, 0, 0, share, right, xt_ref), push(1, 1, 0, 0, share, left, xt_ref), push(2, 2, 0, 0, share, across, xt_ref)]
@@ -191,24 +216,12 @@
     for step in range(1, chips):
         mom_copy(step).start()
 
-    turned[...] = jnp.zeros_like(turned)
-
-    def turn(index, carry):
-        part, quad = lax.div(index, 2), lax.rem(index, 2)
-        for p in range(FIVE):
-            for r in range(4):
-                picks = picks_ref[quad * 4 + r, part * FIVE + p]
-                turned[p * 16:p * 16 + picks.shape[0], r * HALF:(r + 1) * HALF] = (picks & (LANES - 1)).astype(F32)
-        flat = turned[...].T
-        for r in range(4):
-            off_all[quad * 4 + r, part] = flat[r * HALF:(r + 1) * HALF]
-        return carry
-
-    lax.fori_loop(0, chips * 2, turn, 0)
     off_copy = pltpu.make_async_copy(off_all, off_hbm, out_sem.at[0])
     off_copy.start()
     own_copy.wait()
     g_copy.wait()
+    for copy in small_copies[2:]:
+        copy.wait()
 
     second_pushes = [
         push(3, 3, 1, 0, half, right), push(4, 4, 2, half, half, left),
@@ -289,7 +302,7 @@
 
 def grad_chunk(xt, g, mom, off, rowf_ref, rowi_ref, lanef_ref, lanei_ref, exp_ref, comp_ref, new, moved_ref, base):
     rows = pl.ds(base, CHUNK)
-    moved_ref[...] = dot(xt[rows, :], g[...]) + DECAY * mom[rows, :].astype(F32)
+    moved_ref[...] = dot(xt[rows, :], g[...]) * (1.0 / math.sqrt(ROWS)) + DECAY * mom[rows, :].astype(F32)
     off = jnp.concatenate([off] * FIVE, axis=0)
     slots = own_slots((FIVE * HALF, LANES))
     off = jnp.where(slots, off, 0.0).astype(BF)
@@ -318,31 +331,31 @@
     return sum(values[p * HALF:(p + 1) * HALF] for p in range(FIVE))
 
 
-def update_kernel(val_ref, off_ref, rowi_ref, lanei_ref, exp_ref, exp2_ref, same_ref, new_in, up_ref, new_out, even_ref, odd_ref, sem):
-    keep = pltpu.make_async_copy(new_in, new_out, sem)
-
-    @pl.when(pl.program_id(0) == 0)
-    def _():
-        keep.start()
-
+def update_kernel(val_ref, off_ref, rowi_ref, lanei_ref, exp_ref, exp2_ref, same_ref, new_in, up_ref, new_out, even_ref, odd_ref, offs_ref, vals_ref):
+    new_out[...] = new_in[...]
     groups = val_ref.shape[0]
-    slots = own_slots((FIVE * HALF, LANES))
-    even_ref[...] = jnp.zeros_like(even_ref)
-    odd_ref[...] = jnp.zeros_like(odd_ref)
-    lane = lane_in_block(even_ref.shape)
-
-    def add_group(r, carry):
+    width = even_ref.shape[1]
+    rows = FIVE * HALF
+    slots = own_slots((rows, LANES))
+    for r in range(groups):
+        cut = slice(r * rows, (r + 1) * rows)
         off = jnp.concatenate([off_ref[r, 0]] * FIVE, axis=0)
-        off = jnp.where(slots, off, 0.0).astype(BF)
-        offsets = dot(off, exp_ref[...])
-        val = jnp.where(slots, jnp.concatenate([val_ref[r, 0]] * FIVE, axis=0), 0.0)
-        high, low = split(val)
-        values = dot(jnp.concatenate([high, low], axis=1), exp2_ref[...])
-        even_ref[...] += jnp.where(offsets == lane, values, 0.0)
-        odd_ref[...] += jnp.where(offsets == lane + BLOCK, values, 0.0)
-        return carry
-
-    lax.fori_loop(0, groups, add_group, 0)
+        offs_ref[cut, :] = jnp.where(slots, off, 0.0).astype(BF)
+        high, low = split(jnp.where(slots, jnp.concatenate([val_ref[r, 0]] * FIVE, axis=0), 0.0))
+        vals_ref[cut, :LANES] = high
+        vals_ref[cut, LANES:] = low
+    for start in range(0, width, 2 * LANES):
+        lanes = slice(start, min(start + 2 * LANES, width))
+        offsets = dot(offs_ref[...], exp_ref[:, lanes])
+        values = dot(vals_ref[...], exp2_ref[:, lanes])
+        lane = lane_in_block((rows, offsets.shape[1]))
+        even = odd = jnp.zeros(lane.shape, F32)
+        for r in range(groups):
+            off, val = offsets[r * rows:(r + 1) * rows], values[r * rows:(r + 1) * rows]
+            even = even + jnp.where(off == lane, val, 0.0)
+            odd = odd + jnp.where(off == lane + BLOCK, val, 0.0)
+        even_ref[:, lanes] = even
+        odd_ref[:, lanes] = odd
     even, odd = even_ref[...], odd_ref[...]
     squares = even * even + odd * odd
     high, low = split(even)
@@ -362,10 +375,6 @@
         scale = lax.rsqrt(power * (1.0 / (BLOCK * BLOCK)) + EPSILON)
         up_ref[p * BLOCK:(p + 1) * BLOCK, :] = (field * scale).astype(BF)
 
-    @pl.when(pl.program_id(0) == pl.num_programs(0) - 1)
-    def _():
-        keep.wait()
-
 
 def whole(shape):
     return pl.BlockSpec(shape, lambda i: (0,) * len(shape))
@@ -375,31 +384,30 @@
     features, width = mom.shape
     reps = picks.shape[0]
     chunks = features // CHUNK
-    names = ("row_fwd", "row_inv", "lane_fwd", "lane_inv", "expand", "compress")
-    vmem, any_space = pl.BlockSpec(memory_space=pltpu.VMEM), pl.BlockSpec(memory_space=pl.ANY)
+    small = [picks] + [t[n] for n in NAMES]
+    any_space = pl.BlockSpec(memory_space=pl.ANY)
     dma = pltpu.SemaphoreType.DMA
     return pl.pallas_call(
         gather_kernel,
-        in_specs=[any_space, any_space, any_space] + [vmem] * (1 + len(names)),
+        in_specs=[any_space] * (3 + len(small)),
         out_specs=[any_space] * 3,
         out_shape=[
             jax.ShapeDtypeStruct((features, width), BF),
             jax.ShapeDtypeStruct((reps, chunks, HALF, LANES), F32),
             jax.ShapeDtypeStruct((reps, chunks, HALF, LANES), F32),
         ],
-        scratch_shapes=[
+        scratch_shapes=[pltpu.VMEM(a.shape, a.dtype) for a in small] + [
             pltpu.VMEM((features, ROWS), BF),
             pltpu.VMEM(g.shape, BF),
             pltpu.VMEM((features, width), BF),
             pltpu.VMEM((features, width), BF),
             pltpu.VMEM((CHUNK, width), F32),
-            pltpu.VMEM((LANES, LANES), F32),
             pltpu.VMEM((reps, chunks, HALF, LANES), F32),
             pltpu.VMEM((reps, chunks, HALF, LANES), F32),
-            dma, dma((chunks,)), dma((chunks,)), dma((1 + chunks,)), dma, dma((9,)), dma((9,)), dma((chunks,)), dma((chunks,)), dma((3, reps)), dma((3, reps)),
+            dma((len(small),)), dma, dma((chunks,)), dma((chunks,)), dma((1 + chunks,)), dma, dma((9,)), dma((9,)), dma((chunks,)), dma((chunks,)), dma((3, reps)), dma((3, reps)),
         ],
         compiler_params=pltpu.CompilerParams(vmem_limit_bytes=56 * 2**20, collective_id=0, has_side_effects=True),
-    )(xt, g, mom, picks, *(t[n] for n in names))
+    )(xt, g, mom, *small)
 
 
 def update_call(values, off, new, t, width):
@@ -411,19 +419,19 @@
         in_specs=[
             pl.BlockSpec((groups, 1, HALF, LANES), lambda i: (0, i, 0, 0)),
             pl.BlockSpec((groups, 1, HALF, LANES), lambda i: (0, i, 0, 0)),
-        ] + [whole(t[n].shape) for n in names] + [pl.BlockSpec(memory_space=pl.ANY)],
-        out_specs=[pl.BlockSpec((CHUNK, width), lambda i: (i, 0)), pl.BlockSpec(memory_space=pl.ANY)],
+        ] + [whole(t[n].shape) for n in names] + [pl.BlockSpec((CHUNK, width), lambda i: (i, 0))],
+        out_specs=[pl.BlockSpec((CHUNK, width), lambda i: (i, 0))] * 2,
         out_shape=[jax.ShapeDtypeStruct((chunks * CHUNK, width), BF), jax.ShapeDtypeStruct(new.shape, BF)],
-        scratch_shapes=[pltpu.VMEM((FIVE * HALF, width), F32), pltpu.VMEM((FIVE * HALF, width), F32), pltpu.SemaphoreType.DMA],
+        scratch_shapes=[pltpu.VMEM((FIVE * HALF, width), F32), pltpu.VMEM((FIVE * HALF, width), F32), pltpu.VMEM((groups * FIVE * HALF, LANES), BF), pltpu.VMEM((groups * FIVE * HALF, 2 * LANES), BF)],
         compiler_params=pltpu.CompilerParams(vmem_limit_bytes=50 * 2**20),
     )(values, off, *(t[n] for n in names), new)
 
 
 def body(tokens, output_grads, momentum, component_picks):
     width = momentum.shape[2]
-    t = {name: jnp.asarray(table) for name, table in tables(width).items()}
-    xt = (tokens * BF(1.0 / math.sqrt(ROWS))).T
-    new_momentum, values, off = gather_call(xt, output_grads, momentum[0], component_picks, t)
+    t = {name: jnp.asarray(table) for name, table in tables(width, component_picks.shape[1]).items()}
+    picks = jnp.transpose(component_picks, (0, 2, 3, 1))
+    new_momentum, values, off = gather_call(tokens.T, output_grads, momentum[0], picks, t)
     update, new_momentum = update_call(values, off, new_momentum, t, width)
     return (new_momentum[None], update)
 

time: 198 us -> 77.4 us (0.39)
  Pallas kernels: 189 us -> 73.1 us
  local copies, waits for them, and re-layouts: 5.73 us -> 2.48 us
    pallas_call x1, Pallas kernels: 141 us -> 24.8 us  [update_call(): pl.pallas_call(update_kernel, grid=(chunks,), in_specs=[pl.BlockSpec((gro...]
    unnamed x15 -> x14, local copies, waits for them, and re-layouts: 5.73 us -> 2.48 us
where the time goes in v3:
time: 77.4 us; the launch traced here: 76.3 us
  Pallas kernels  73.1 us (94%)
  local copies, waits for them, and re-layouts  2.48 us (3%)
    pallas_call x1, Pallas kernels, gather_call(): pl.pallas_call(gather_kernel, in_specs=[any_space] * (3 + len(small)), ou...  48.3 us
    pallas_call x1, Pallas kernels, update_call(): pl.pallas_call(update_kernel, grid=(chunks,), in_specs=[pl.BlockSpec((gro...  24.8 us
    unnamed x14, local copies, waits for them, and re-layouts  2.48 us

profile of v3, /device:TPU:1, one launch (start us, length us, event | category | flops | bytes accessed | tf_op | source)
XLA Modules:
  0.0 76.3 jit_solution(10316595188968942836)
XLA Ops:
  0.6 0.0 copy-start.2
  0.6 0.0 copy-start.3
  0.7 0.0 copy-start.4
  0.7 0.0 copy-start.5
  0.7 0.0 copy-start.6
  0.7 48.3 %shard_map.140 = (bf16[2560,896]{1,0:T(8,128)(2,1)}, f32[8,8,32,128]{3,2,1,0:T(8,128)}, f32[8,8,32,128]{3,2,1,0:T(8,128)}) custom-call(bf16[160,1024]{1,0:T(8,128)(2,1)} %bitcast.6, bf16[1024,896]{1,0:T(8,128)(2,1)} %g_hbm.1, bf16[2560,896]{1,0:T(8,128)(2,1)} %bitcast.4, s32[8,14,32,40]{3,2,1,0:T(8,128)} %bitcast.5, ...), custom_call_target="tpu_custom_call" | custom-call | tf_op jit(solution)/shard_map/pallas_call | solution.py:390
  49.0 0.0 copy-done.2
  49.0 0.0 copy-done.3
  49.0 0.0 copy-done.4
  49.0 0.0 copy-done.5
  49.0 0.0 copy-done.6
  49.0 0.0 copy-start
  49.0 1.2 %copy-done = f32[8,8,32,128]{3,2,1,0:T(8,128)S(1)} copy-done((f32[8,8,32,128]{3,2,1,0:T(8,128)S(1)}, f32[8,8,32,128]{3,2,1,0:T(8,128)}, u32[]{:S(2)}) %copy-start) | copy-done | bytes 1048600
  50.2 0.0 copy-start.1
  50.2 1.2 %copy-done.1 = f32[8,8,32,128]{3,2,1,0:T(8,128)S(1)} copy-done((f32[8,8,32,128]{3,2,1,0:T(8,128)S(1)}, f32[8,8,32,128]{3,2,1,0:T(8,128)}, u32[]{:S(2)}) %copy-start.1) | copy-done | bytes 1048600
  51.5 24.8 %shard_map.141 = (bf16[2560,896]{1,0:T(8,128)(2,1)}, bf16[2560,896]{1,0:T(8,128)(2,1)}) custom-call(f32[8,8,32,128]{3,2,1,0:T(8,128)S(1)} %copy-done, f32[8,8,32,128]{3,2,1,0:T(8,128)S(1)} %copy-done.1, bf16[64,192]{1,0:T(8,128)(2,1)S(1)} %copy-done.5, bf16[256,256]{1,0:T(8,128)(2,1)S(1)} %copy-done.3, bf16[128,896]{1,0:T(8,128)(2,1)S(1)} %copy-done.2, ...), custom_call_target="tpu_custom_call" | custom-call | tf_op jit(solution)/shard_map/pallas_call | solution.py:416
Async XLA Ops:
  0.6 48.3 %copy-start.2 = (bf16[128,896]{1,0:T(8,128)(2,1)S(1)}, bf16[128,896]{1,0:T(8,128)(2,1)}, u32[]{:S(2)}) copy-start(bf16[128,896]{1,0:T(8,128)(2,1)} %constant.23.clone.refs_6_.exp_ref) | copy-start | bytes 688132
  0.6 48.3 %copy-start.3 = (bf16[256,256]{1,0:T(8,128)(2,1)S(1)}, bf16[256,256]{1,0:T(8,128)(2,1)}, u32[]{:S(2)}) copy-start(bf16[256,256]{1,0:T(8,128)(2,1)} %constant.22.clone.refs_5_.lanei_ref) | copy-start | bytes 393220
  0.7 48.3 %copy-start.4 = (bf16[256,896]{1,0:T(8,128)(2,1)S(1)}, bf16[256,896]{1,0:T(8,128)(2,1)}, u32[]{:S(2)}) copy-start(bf16[256,896]{1,0:T(8,128)(2,1)} %constant.24.clone.exp2_ref) | copy-start | bytes 1376260
  0.7 48.3 %copy-start.5 = (bf16[64,192]{1,0:T(8,128)(2,1)S(1)}, bf16[64,192]{1,0:T(8,128)(2,1)}, u32[]{:S(2)}) copy-start(bf16[64,192]{1,0:T(8,128)(2,1)} %constant.20.clone.refs_3_.rowi_ref) | copy-start | bytes 73732
  0.7 48.3 %copy-start.6 = (bf16[128,128]{1,0:T(8,128)(2,1)S(1)}, bf16[128,128]{1,0:T(8,128)(2,1)}, u32[]{:S(2)}) copy-start(bf16[128,128]{1,0:T(8,128)(2,1)} %constant.26.clone.same_ref) | copy-start | bytes 98308
  49.0 1.2 %copy-start = (f32[8,8,32,128]{3,2,1,0:T(8,128)S(1)}, f32[8,8,32,128]{3,2,1,0:T(8,128)}, u32[]{:S(2)}) copy-start(f32[8,8,32,128]{3,2,1,0:T(8,128)} %get-tuple-element.7.val_ref) | copy-start | bytes 3145732
  50.2 1.2 %copy-start.1 = (f32[8,8,32,128]{3,2,1,0:T(8,128)S(1)}, f32[8,8,32,128]{3,2,1,0:T(8,128)}, u32[]{:S(2)}) copy-start(f32[8,8,32,128]{3,2,1,0:T(8,128)} %get-tuple-element.8.off_ref) | copy-start | bytes 3145732

commit v4 on v3

v4 whole, which is shorter than its diff:
```python
import functools
import math

import jax
import jax.numpy as jnp
import ml_dtypes
import numpy as np
from jax import lax
from jax.experimental import pallas as pl
from jax.experimental.pallas import tpu as pltpu
from jax.sharding import PartitionSpec as P

ROWS = 1024
BLOCK = 64
HALF = 32
FIVE = 5
CHUNK = FIVE * BLOCK
LANES = 128
SLOT = 8
QUAD = 4
LISTED = 16
DECAY = 0.9
EPSILON = 1e-06
NAMES = ("select", "row_fwd", "row_inv", "lane_fwd", "lane_inv", "expand", "compress")
BF = jnp.bfloat16
F32 = jnp.float32


def split_table(table):
    high = table.astype(ml_dtypes.bfloat16)
    low = (table - high.astype(np.float64)).astype(ml_dtypes.bfloat16)
    return high, low


def tables(width, width_rows):
    frequency = np.arange(BLOCK, dtype=np.float64)[:, None]
    position = np.arange(BLOCK, dtype=np.float64)[None, :]
    norm = np.where(frequency == 0, math.sqrt(1.0 / BLOCK), math.sqrt(2.0 / BLOCK))
    cosine = norm * np.cos(math.pi * (2.0 * position + 1.0) * frequency / (2.0 * BLOCK))
    ordered = np.concatenate([cosine[0::2], cosine[1::2]])

    def rows_table(matrix):
        high, low = split_table(matrix)
        return np.concatenate([high, high, low], axis=1)

    def lanes_table(matrix):
        pair = np.zeros((LANES, LANES))
        pair[:BLOCK, :BLOCK] = matrix
        pair[BLOCK:, BLOCK:] = matrix
        high, low = split_table(pair)
        return np.concatenate(
            [np.concatenate([high, low], axis=1), np.concatenate([high, np.zeros_like(low)], axis=1)]
        )

    slot = np.arange(LANES)[:, None] // SLOT
    block = np.arange(width)[None, :] // BLOCK
    expand = (slot == block).astype(ml_dtypes.bfloat16)
    rows = width_rows
    select = np.zeros((width // BLOCK, rows, rows // FIVE * LANES), ml_dtypes.bfloat16)
    for b in range(width // BLOCK):
        for p in range(rows):
            select[b, p, p // FIVE * LANES + b * SLOT + p % FIVE] = 1.0
    high, low = split_table(cosine.T)
    columns = np.concatenate([high, high, low], axis=1)
    spread = np.zeros((QUAD, BLOCK, 2, QUAD, HALF))
    for p in range(QUAD):
        for parity in range(2):
            spread[p, :, parity, p, :] = cosine[parity::2].T
    high, low = split_table(spread.reshape(QUAD * BLOCK, 2 * QUAD * HALF))
    segment = (np.arange(LANES)[:, None] // HALF == np.arange(LANES)[None, :] // HALF).astype(ml_dtypes.bfloat16)
    return {
        "select": select,
        "row_fwd": rows_table(ordered),
        "row_inv": rows_table(ordered.T),
        "lane_fwd": lanes_table(cosine.T),
        "lane_inv": lanes_table(cosine),
        "expand": expand,
        "compress": (np.arange(LISTED)[:, None] == block).astype(ml_dtypes.bfloat16),
        "columns": columns,
        "spread": np.concatenate([high, low]),
        "segment": np.concatenate([segment, segment]),
    }


def dot(a, b):
    return jnp.dot(a, b, preferred_element_type=F32)


def dot_t(a, b):
    return lax.dot_general(a, b, (((1,), (1,)), ((), ())), preferred_element_type=F32)


def split(value):
    high = value.astype(BF)
    return high, (value - high.astype(F32)).astype(BF)


def lane_transform(high, low, weights):
    groups = high.shape[1] // LANES
    parts = []
    for group in range(groups):
        cut = slice(group * LANES, (group + 1) * LANES)
        both = dot(jnp.concatenate([high[:, cut], low[:, cut]], axis=1), weights)
        parts.append(both[:, :LANES] + both[:, LANES:])
    return jnp.concatenate(parts, axis=1)


def own_slots(shape):
    row = lax.broadcasted_iota(jnp.int32, shape, 0) // HALF
    lane = lax.broadcasted_iota(jnp.int32, shape, 1) % SLOT
    return lane == row


def lane_in_block(shape):
    return (lax.broadcasted_iota(jnp.int32, shape, 1) % BLOCK).astype(F32)


def gather_kernel(xt_ref, g_hbm, mom_hbm, *refs):
    count = len(NAMES) + 1
    small_hbm, refs = refs[:count], refs[count:]
    new_hbm, val_hbm, off_hbm = refs[:3]
    small, refs = refs[3:3 + count], refs[3 + count:]
    picks_ref, select_ref, rowf_ref, rowi_ref, lanef_ref, lanei_ref, exp_ref, comp_ref = small
    (xt, g, mom, new, moved, picked_high, picked_low, turned, flipped, off_own, off_all, val_all,
                  small_sem, g_sem, mom_sem, new_sem, out_sem, own_sem, send_sem, recv_sem, pass_sem, sib_sem, vsend_sem, vrecv_sem) = refs
    share = xt_ref.shape[0]
    chips = mom.shape[0] // CHUNK
    line = chips // 2
    reps = val_all.shape[0]
    rep, tp = lax.axis_index("rep"), lax.axis_index("tp")
    core, chip = lax.rem(tp, 2), lax.div(tp, 2)
    x, y = lax.rem(chip, line), lax.div(chip, line)

    def chip_at(dx, dy):
        return lax.rem(y + dy, 2) * line + lax.rem(x + dx, line)

    def device_at(dx, dy):
        return {"tp": chip_at(dx, dy) * 2 + core}

    left, right, across, sibling = device_at(line - 1, 0), device_at(1, 0), device_at(0, 1), {"tp": chip * 2 + 1 - core}

    def chip_of(step):
        dy = jnp.where((step == 3) | (step >= 5), 1, 0)
        dx = jnp.where((step == 1) | (step == 5), line - 1, jnp.where((step == 2) | (step == 6), 1, jnp.where((step == 4) | (step == 7), 2, 0)))
        return chip_at(dx, dy)

    def rows_of(step, first, count):
        start = (chip_of(step) * 2 + core) * share + first
        return xt.at[pl.ds(pl.multiple_of(start, 16), count), :]

    half = share // 2

    def push(index, recv, step, first, count, target, source=None):
        rows = rows_of(step, first, count)
        return pltpu.make_async_remote_copy(
            src_ref=rows if source is None else source, dst_ref=rows,
            send_sem=send_sem.at[index], recv_sem=recv_sem.at[recv],
            device_id=target, device_id_type=pl.DeviceIdType.MESH)

    def arrive(recv, step, first, count):
        push(0, recv, step, first, count, left).wait_recv()

    def to_sibling(step, source=None):
        rows = rows_of(step, 0, share)
        return pltpu.make_async_remote_copy(
            src_ref=rows if source is None else source, dst_ref=rows,
            send_sem=pass_sem.at[step], recv_sem=sib_sem.at[step],
            device_id=sibling, device_id_type=pl.DeviceIdType.MESH)

    def from_sibling(step):
        start = (chip_of(step) * 2 + 1 - core) * share
        rows = xt.at[pl.ds(pl.multiple_of(start, 16), share), :]
        pltpu.make_async_remote_copy(
            src_ref=rows, dst_ref=rows, send_sem=pass_sem.at[step], recv_sem=sib_sem.at[step],
            device_id=sibling, device_id_type=pl.DeviceIdType.MESH).wait_recv()

    def mom_copy(step):
        rows = pl.ds(pl.multiple_of(chip_of(step) * CHUNK, CHUNK), CHUNK)
        return pltpu.make_async_copy(mom_hbm.at[rows, :], mom.at[rows, :], mom_sem.at[step])

    def new_copy(step):
        rows = pl.ds(pl.multiple_of(chip_of(step) * CHUNK, CHUNK), CHUNK)
        return pltpu.make_async_copy(new.at[rows, :], new_hbm.at[rows, :], new_sem.at[step])

    def send_values(step, ahead):
        slab = val_all.at[rep, step]
        return pltpu.make_async_remote_copy(
            src_ref=slab, dst_ref=slab,
            send_sem=vsend_sem.at[step, ahead], recv_sem=vrecv_sem.at[step, ahead],
            device_id={"rep": lax.rem(rep + ahead, reps)}, device_id_type=pl.DeviceIdType.MESH)

    def take_values(step, behind):
        slab = val_all.at[lax.rem(rep + reps - behind, reps), step]
        return pltpu.make_async_remote_copy(
            src_ref=slab, dst_ref=slab,
            send_sem=vsend_sem.at[step, behind], recv_sem=vrecv_sem.at[step, behind],
            device_id={"rep": lax.rem(rep + behind, reps)}, device_id_type=pl.DeviceIdType.MESH)

    own_rows = rows_of(0, 0, share)
    own_copy = pltpu.make_async_copy(xt_ref, own_rows, own_sem)
    own_copy.start()
    small_copies = [pltpu.make_async_copy(small_hbm[n], small[n], small_sem.at[n]) for n in range(count)]
    for copy in small_copies:
        copy.start()
    g_copy = pltpu.make_async_copy(g_hbm, g, g_sem)
    g_copy.start()
    mom_copy(0).start()

    barrier = pltpu.get_barrier_semaphore()
    for target in (left, right, across, sibling):
        pl.semaphore_signal(barrier, inc=1, device_id=target, device_id_type=pl.DeviceIdType.MESH)
    for ahead in range(1, reps):
        pl.semaphore_signal(barrier, inc=1, device_id={"rep": lax.rem(rep + ahead, reps)}, device_id_type=pl.DeviceIdType.MESH)
    pl.semaphore_wait(barrier, 4 + reps - 1)

    own_low, own_high = xt_ref.at[pl.ds(0, half), :], xt_ref.at[pl.ds(half, half), :]
    first_pushes = [
        push(0, 0, 0, 0, half, right, own_low), push(1, 1, 0, half, half, left, own_high), push(2, 2, 0, 0, half, across, own_low),
        push(3, 3, 0, half, half, right, own_high), push(4, 4, 0, 0, half, left, own_low), push(5, 5, 0, half, half, across, own_high)]
    to_sibling(0, xt_ref).start()
    for copy in first_pushes:
        copy.start()
    for step in range(1, chips):
        mom_copy(step).start()

    small_copies[0].wait()
    small_copies[1].wait()
    blocks = picks_ref.shape[1]
    flat = jnp.zeros((HALF, chips * LANES), F32)
    for b in range(blocks):
        low_bits = (picks_ref[rep, b] & (LANES - 1)).astype(F32).astype(BF)
        flat = flat + dot(low_bits, select_ref[b])
    for part in range(chips):
        off_own[part] = flat[:, part * LANES:(part + 1) * LANES]
    own_copy.wait()
    g_copy.wait()
    for copy in small_copies[2:]:
        copy.wait()

    turned[...] = jnp.zeros_like(turned)

    def turn(r, carry):
        for first in range(0, blocks, QUAD):
            for place in range(min(QUAD, blocks - first)):
                turned[place * HALF:(place + 1) * HALF, :picks_ref.shape[3]] = (picks_ref[r, first + place] & (LANES - 1)).astype(F32)
            flipped[...] = turned[...].T
            for p in range(QUAD):
                lines = flipped[pl.ds(p, off_all.shape[2], stride=QUAD), :]
                for place in range(min(QUAD, blocks - first)):
                    off_all[r, first + place, :, p * HALF:(p + 1) * HALF] = lines[:, place * HALF:(place + 1) * HALF]
        return carry

    second_pushes = [
        push(6, 6, 1, 0, half, right), push(7, 7, 2, half, half, left),
        push(8, 8, 3, 0, share, right), push(9, 9, 3, 0, share, left)]
    third_pushes = [push(10, 10, 4, 0, half, across), push(11, 11, 4, half, half, across)]

    def forward(step):
        chunk = chip_of(step)
        grad_chunk(xt, g, mom, off_own[chunk], rowf_ref, lanef_ref, exp_ref, comp_ref, moved, picked_high, picked_low,
                   val_all.at[rep, step], chunk)

    def backward(step):
        chunk = chip_of(step)
        back_chunk(off_own[chunk], rowi_ref, lanei_ref, exp_ref, moved, picked_high, picked_low, new, chunk)
        new_copy(step).start()

    def backward_step(step, carry):
        backward(step)
        return carry

    def one(step, carry):
        @pl.when(step == 1)
        def _():
            arrive(0, 1, 0, half)
            second_pushes[0].start()
            arrive(1, 2, half, half)
            second_pushes[1].start()
            lax.fori_loop(0, reps, turn, 0)
            pltpu.make_async_copy(off_all, off_hbm, out_sem.at[0]).start()
            arrive(2, 3, 0, half)
            arrive(5, 3, half, half)
            second_pushes[2].start()
            second_pushes[3].start()
            arrive(3, 1, half, half)
            to_sibling(1).start()
            arrive(4, 2, 0, half)
            to_sibling(2).start()
            to_sibling(3).start()

        @pl.when(step == 2)
        def _():
            arrive(6, 4, 0, half)
            third_pushes[0].start()
            arrive(7, 4, half, half)
            third_pushes[1].start()
            to_sibling(4).start()

        @pl.when(step == 5)
        def _():
            lax.fori_loop(0, 4, backward_step, 0)
            arrive(8, 5, 0, share)
            to_sibling(5).start()
            arrive(9, 6, 0, share)
            to_sibling(6).start()
            arrive(10, 7, 0, half)
            arrive(11, 7, half, half)
            to_sibling(7).start()
            lax.fori_loop(4, 5, backward_step, 0)

        from_sibling(step)
        mom_copy(step).wait()
        forward(step)
        for ahead in range(1, reps):
            send_values(step, ahead).start()
        return carry

    lax.fori_loop(0, chips, one, 0)
    lax.fori_loop(5, chips, backward_step, 0)
    for copy in first_pushes + second_pushes + third_pushes:
        copy.wait_send()

    def settle(step, carry):
        to_sibling(step).wait_send()
        for behind in range(1, reps):
            take_values(step, behind).wait_recv()
        pltpu.make_async_copy(val_all.at[:, step], val_hbm.at[:, chip_of(step)], out_sem.at[1 + step]).start()
        return carry

    def finish(step, carry):
        for ahead in range(1, reps):
            send_values(step, ahead).wait_send()
        new_copy(step).wait()
        pltpu.make_async_copy(val_all.at[:, step], val_hbm.at[:, chip_of(step)], out_sem.at[1 + step]).wait()
        return carry

    lax.fori_loop(0, chips, settle, 0)
    lax.fori_loop(0, chips, finish, 0)
    pltpu.make_async_copy(off_all, off_hbm, out_sem.at[0]).wait()


def spread_offsets(off, exp_ref):
    off = jnp.where(own_slots((FIVE * HALF, LANES)), jnp.concatenate([off] * FIVE, axis=0), 0.0).astype(BF)
    return dot(off, exp_ref[...])


def grad_chunk(xt, g, mom, off, rowf_ref, lanef_ref, exp_ref, comp_ref, moved_ref, high_ref, low_ref, val_ref, chunk):
    rows = pl.ds(pl.multiple_of(chunk * CHUNK, CHUNK), CHUNK)
    half_rows = pl.ds(pl.multiple_of(chunk * (CHUNK // 2), CHUNK // 2), CHUNK // 2)
    moved = moved_ref.at[rows, :]
    moved[...] = dot(xt[rows, :], g[...]) * (1.0 / math.sqrt(ROWS)) + DECAY * mom[rows, :].astype(F32)
    offsets = spread_offsets(off, exp_ref)
    odd = offsets >= BLOCK
    picked_rows = []
    for p in range(FIVE):
        high, low = split(moved[p * BLOCK:(p + 1) * BLOCK, :])
        freq = dot(rowf_ref[...], jnp.concatenate([high, low, high], axis=0))
        cut = slice(p * HALF, (p + 1) * HALF)
        picked_rows.append(jnp.where(odd[cut], freq[HALF:], freq[:HALF]))
    high, low = split(jnp.concatenate(picked_rows, axis=0))
    spectrum = lane_transform(high, low, lanef_ref[...])
    column = jnp.where(odd, offsets - BLOCK, offsets)
    high, low = split(jnp.where(column == lane_in_block(offsets.shape), spectrum, 0.0))
    high_ref[half_rows, :] = high
    low_ref[half_rows, :] = low
    val_ref[:, :FIVE * HALF] = dot_t(comp_ref[...], high) + dot_t(comp_ref[...], low)


def back_chunk(off, rowi_ref, lanei_ref, exp_ref, moved_ref, high_ref, low_ref, new, chunk):
    base = pl.multiple_of(chunk * CHUNK, CHUNK)
    half_rows = pl.ds(pl.multiple_of(chunk * (CHUNK // 2), CHUNK // 2), CHUNK // 2)
    odd = spread_offsets(off, exp_ref) >= BLOCK
    spread = lane_transform(high_ref[half_rows, :], low_ref[half_rows, :], lanei_ref[...])
    for p in range(FIVE):
        cut = slice(p * HALF, (p + 1) * HALF)
        part = spread[cut]
        high, low = split(jnp.concatenate([jnp.where(odd[cut], 0.0, part), jnp.where(odd[cut], part, 0.0)], axis=0))
        taken = dot(rowi_ref[...], jnp.concatenate([high, low, high], axis=0))
        rows = pl.ds(base + p * BLOCK, BLOCK)
        new[rows, :] = (moved_ref[rows, :] - taken).astype(BF)


def update_kernel(val_ref, off_ref, col_ref, spread_ref, seg_ref, new_in, up_ref, new_out, vals, sums, high_ref, low_ref):
    step = pl.program_id(0)
    groups, blocks = off_ref.shape[:2]
    chips = val_ref.shape[1]
    new_out[...] = new_in[...]

    @pl.when(step == 0)
    def _():
        for r in range(groups):
            line = jnp.concatenate([val_ref[r, c][:, :FIVE * HALF] for c in range(chips)], axis=1)
            for i in range(line.shape[1] // LANES):
                vals[i, r] = line[:, i * LANES:(i + 1) * LANES]

    column = lax.broadcasted_iota(jnp.int32, (BLOCK, LANES), 0).astype(F32)
    powers = []
    for b in range(blocks):
        even = odd = jnp.zeros((BLOCK, LANES), F32)
        for r in range(groups):
            line = off_ref[r, b, pl.ds(step, 1), :]
            val = jnp.broadcast_to(vals[step, r, b:b + 1, :], (BLOCK, LANES))
            even = even + jnp.where(jnp.broadcast_to(line, (BLOCK, LANES)) == column, val, 0.0)
            odd = odd + jnp.where(jnp.broadcast_to(line - BLOCK, (BLOCK, LANES)) == column, val, 0.0)
        sums[b, :, :LANES] = even
        sums[b, :, LANES:] = odd
        powers.append(jnp.sum(even * even + odd * odd, axis=0, keepdims=True))
    powers = jnp.concatenate(powers + [jnp.zeros((16 - blocks, LANES), F32)], axis=0)
    high, low = split(powers)
    power = dot(jnp.concatenate([high, low], axis=1), seg_ref[...])
    scale = lax.rsqrt(power * (1.0 / (BLOCK * BLOCK)) + EPSILON)
    for b in range(blocks):
        row = jnp.concatenate([scale[b:b + 1]] * 2, axis=1)
        high, low = split(sums[b] * row)
        half = dot(col_ref[...], jnp.concatenate([high, low, high], axis=0))
        high, low = split(half)
        high_ref[b * BLOCK:(b + 1) * BLOCK, :] = high
        low_ref[b * BLOCK:(b + 1) * BLOCK, :] = low
    rows = QUAD * BLOCK
    width = high_ref.shape[0]
    for start in range(0, width, 256):
        cut = slice(start, min(start + 256, width))
        field = dot_t(spread_ref[:rows], high_ref[cut]) + dot_t(spread_ref[rows:], high_ref[cut]) + dot_t(spread_ref[:rows], low_ref[cut])
        up_ref[:, cut] = field.astype(BF)


def whole(shape):
    return pl.BlockSpec(shape, lambda i: (0,) * len(shape))


def gather_call(xt, g, mom, picks, t):
    features, width = mom.shape
    reps = picks.shape[0]
    chunks = features // CHUNK
    values = (reps, chunks, LISTED, 2 * LANES)
    offsets = (reps, picks.shape[1], features // (QUAD * BLOCK), LANES)
    small = [picks] + [t[n] for n in NAMES]
    any_space = pl.BlockSpec(memory_space=pl.ANY)
    dma = pltpu.SemaphoreType.DMA
    return pl.pallas_call(
        gather_kernel,
        in_specs=[any_space] * (3 + len(small)),
        out_specs=[any_space] * 3,
        out_shape=[
            jax.ShapeDtypeStruct((features, width), BF),
            jax.ShapeDtypeStruct(values, F32),
            jax.ShapeDtypeStruct(offsets, F32),
        ],
        scratch_shapes=[pltpu.VMEM(a.shape, a.dtype) for a in small] + [
            pltpu.VMEM((features, ROWS), BF),
            pltpu.VMEM(g.shape, BF),
            pltpu.VMEM((features, width), BF),
            pltpu.VMEM((features, width), BF),
            pltpu.VMEM((features, width), F32),
            pltpu.VMEM((features // 2, width), BF),
            pltpu.VMEM((features // 2, width), BF),
            pltpu.VMEM((LANES, LANES), F32),
            pltpu.VMEM((LANES, LANES), F32),
            pltpu.VMEM((chunks, HALF, LANES), F32),
            pltpu.VMEM(offsets, F32),
            pltpu.VMEM(values, F32),
            dma((len(small),)), dma, dma((chunks,)), dma((chunks,)), dma((1 + chunks,)), dma, dma((12,)), dma((12,)), dma((chunks,)), dma((chunks,)), dma((chunks, reps)), dma((chunks, reps)),
        ],
        compiler_params=pltpu.CompilerParams(vmem_limit_bytes=56 * 2**20, collective_id=0, has_side_effects=True),
    )(xt, g, mom, *small)


def update_call(values, off, new, t):
    groups, chips = values.shape[:2]
    blocks, steps = off.shape[1:3]
    rows, width = QUAD * BLOCK, blocks * BLOCK
    names = ("columns", "spread", "segment")
    return pl.pallas_call(
        update_kernel, grid=(new.shape[0] // rows,),
        in_specs=[whole(values.shape), whole(off.shape)] + [whole(t[n].shape) for n in names] + [pl.BlockSpec((rows, width), lambda i: (i, 0))],
        out_specs=[pl.BlockSpec((rows, width), lambda i: (i, 0))] * 2,
        out_shape=[jax.ShapeDtypeStruct(new.shape, BF), jax.ShapeDtypeStruct(new.shape, BF)],
        scratch_shapes=[pltpu.VMEM((new.shape[0] // rows, groups, values.shape[2], LANES), F32),
            pltpu.VMEM((blocks, BLOCK, 2 * LANES), F32), pltpu.VMEM((width, 2 * LANES), BF), pltpu.VMEM((width, 2 * LANES), BF)],
        compiler_params=pltpu.CompilerParams(vmem_limit_bytes=60 * 2**20),
    )(values, off, *(t[n] for n in names), new)


def body(tokens, output_grads, momentum, component_picks):
    width = momentum.shape[2]
    t = {name: jnp.asarray(table) for name, table in tables(width, component_picks.shape[1]).items()}
    picks = jnp.transpose(component_picks, (0, 2, 3, 1))
    new_momentum, values, off = gather_call(tokens.T, output_grads, momentum[0], picks, t)
    update, new_momentum = update_call(values, off, new_momentum, t)
    return (new_momentum[None], update)


def solution(mesh):
    return jax.shard_map(
        body,
        mesh=mesh,
        in_specs=(P("rep", "tp"), P("rep", "tp"), P("rep", None, "tp"), P(None, None, "tp", None)),
        out_specs=(P("rep", None, "tp"), P(None, "tp")),
        check_vma=False,
    )
```

time: 77.4 us -> 67.7 us (0.87); the launches traced: 76.3 us -> 67.6 us
  Pallas kernels: 73.1 us -> 67 us
  local copies, waits for them, and re-layouts: 2.48 us -> 0 us
    pallas_call x1, Pallas kernels: 24.8 us -> 21.3 us  [update_call(): pl.pallas_call(update_kernel, grid=(new.shape[0] // rows,), in_specs=[who...]
    pallas_call x1, Pallas kernels: 48.3 us -> 45.7 us  [gather_call(): pl.pallas_call(gather_kernel, in_specs=[any_space] * (3 + len(small)), ou...]
    unnamed x14 -> x0, local copies, waits for them, and re-layouts: 2.48 us -> none
where the time goes in v4:
time: 67.7 us; the launch traced here: 67.6 us
  Pallas kernels  67 us (99%)
    pallas_call x1, Pallas kernels, gather_call(): pl.pallas_call(gather_kernel, in_specs=[any_space] * (3 + len(small)), ou...  45.7 us
    pallas_call x1, Pallas kernels, update_call(): pl.pallas_call(update_kernel, grid=(new.shape[0] // rows,), in_specs=[who...  21.3 us

profile of v4, /device:TPU:1, one launch (start us, length us, event | category | flops | bytes accessed | tf_op | source)
XLA Modules:
  0.0 67.6 jit_solution(18265112197903200339)
XLA Ops:
  0.6 45.7 %shard_map.149 = (bf16[2560,896]{1,0:T(8,128)(2,1)}, f32[8,8,16,256]{3,2,1,0:T(8,128)}, f32[8,14,10,128]{3,2,1,0:T(8,128)}) custom-call(bf16[160,1024]{1,0:T(8,128)(2,1)} %bitcast.6, bf16[1024,896]{1,0:T(8,128)(2,1)} %g_hbm.1, bf16[2560,896]{1,0:T(8,128)(2,1)} %bitcast.4, s32[8,14,32,40]{3,2,1,0:T(8,128)} %bitcast.5, ...), custom_call_target="tpu_custom_call" | custom-call | tf_op jit(solution)/shard_map/pallas_call | solution.py:440
  46.3 21.3 %shard_map.150 = (bf16[2560,896]{1,0:T(8,128)(2,1)}, bf16[2560,896]{1,0:T(8,128)(2,1)}) custom-call(f32[8,8,16,256]{3,2,1,0:T(8,128)} %get-tuple-element.7.val_ref, f32[8,14,10,128]{3,2,1,0:T(8,128)} %get-tuple-element.8.off_ref, bf16[64,192]{1,0:T(8,128)(2,1)} %constant.27.clone.col_ref, bf16[512,256]{1,0:T(8,128)(2,1)} %constant.28.clone.spread_ref, ...), custom_call_target="tpu_custom_call" | custom-call | tf_op jit(solution)/shard_map/pallas_call | solution.py:473

commit v5 on v4

--- a/solution.py
+++ b/solution.py
@@ -160,18 +160,18 @@
     def arrive(recv, step, first, count):
         push(0, recv, step, first, count, left).wait_recv()
 
-    def to_sibling(step, source=None):
-        rows = rows_of(step, 0, share)
+    def to_sibling(step, part, source=None):
+        rows = rows_of(step, part * half, half)
         return pltpu.make_async_remote_copy(
             src_ref=rows if source is None else source, dst_ref=rows,
-            send_sem=pass_sem.at[step], recv_sem=sib_sem.at[step],
+            send_sem=pass_sem.at[step, part], recv_sem=sib_sem.at[step, part],
             device_id=sibling, device_id_type=pl.DeviceIdType.MESH)
 
-    def from_sibling(step):
-        start = (chip_of(step) * 2 + 1 - core) * share
-        rows = xt.at[pl.ds(pl.multiple_of(start, 16), share), :]
+    def from_sibling(step, part):
+        start = (chip_of(step) * 2 + 1 - core) * share + part * half
+        rows = xt.at[pl.ds(pl.multiple_of(start, 16), half), :]
         pltpu.make_async_remote_copy(
-            src_ref=rows, dst_ref=rows, send_sem=pass_sem.at[step], recv_sem=sib_sem.at[step],
+            src_ref=rows, dst_ref=rows, send_sem=pass_sem.at[step, part], recv_sem=sib_sem.at[step, part],
             device_id=sibling, device_id_type=pl.DeviceIdType.MESH).wait_recv()
 
     def mom_copy(step):
@@ -196,6 +196,11 @@
             send_sem=vsend_sem.at[step, behind], recv_sem=vrecv_sem.at[step, behind],
             device_id={"rep": lax.rem(rep + behind, reps)}, device_id_type=pl.DeviceIdType.MESH)
 
+    barrier = pltpu.get_barrier_semaphore()
+    for target in (left, right, across, sibling):
+        pl.semaphore_signal(barrier, inc=1, device_id=target, device_id_type=pl.DeviceIdType.MESH)
+    for ahead in range(1, reps):
+        pl.semaphore_signal(barrier, inc=1, device_id={"rep": lax.rem(rep + ahead, reps)}, device_id_type=pl.DeviceIdType.MESH)
     own_rows = rows_of(0, 0, share)
     own_copy = pltpu.make_async_copy(xt_ref, own_rows, own_sem)
     own_copy.start()
@@ -206,18 +211,14 @@
     g_copy.start()
     mom_copy(0).start()
 
-    barrier = pltpu.get_barrier_semaphore()
-    for target in (left, right, across, sibling):
-        pl.semaphore_signal(barrier, inc=1, device_id=target, device_id_type=pl.DeviceIdType.MESH)
-    for ahead in range(1, reps):
-        pl.semaphore_signal(barrier, inc=1, device_id={"rep": lax.rem(rep + ahead, reps)}, device_id_type=pl.DeviceIdType.MESH)
     pl.semaphore_wait(barrier, 4 + reps - 1)
 
     own_low, own_high = xt_ref.at[pl.ds(0, half), :], xt_ref.at[pl.ds(half, half), :]
     first_pushes = [
         push(0, 0, 0, 0, half, right, own_low), push(1, 1, 0, half, half, left, own_high), push(2, 2, 0, 0, half, across, own_low),
         push(3, 3, 0, half, half, right, own_high), push(4, 4, 0, 0, half, left, own_low), push(5, 5, 0, half, half, across, own_high)]
-    to_sibling(0, xt_ref).start()
+    to_sibling(0, 0, own_low).start()
+    to_sibling(0, 1, own_high).start()
     for copy in first_pushes:
         copy.start()
     for step in range(1, chips):
@@ -250,10 +251,10 @@
                     off_all[r, first + place, :, p * HALF:(p + 1) * HALF] = lines[:, place * HALF:(place + 1) * HALF]
         return carry
 
-    second_pushes = [
-        push(6, 6, 1, 0, half, right), push(7, 7, 2, half, half, left),
-        push(8, 8, 3, 0, share, right), push(9, 9, 3, 0, share, left)]
-    third_pushes = [push(10, 10, 4, 0, half, across), push(11, 11, 4, half, half, across)]
+    later_pushes = {
+        6: push(6, 6, 1, 0, half, right), 7: push(7, 7, 2, half, half, left), 8: push(8, 8, 1, 0, half, across),
+        9: push(9, 9, 3, half, half, right), 10: push(10, 10, 3, 0, half, left), 11: push(11, 11, 2, half, half, across),
+        12: push(12, 12, 4, 0, half, across), 13: push(13, 13, 5, half, half, right)}
 
     def forward(step):
         chunk = chip_of(step)
@@ -272,43 +273,62 @@
     def one(step, carry):
         @pl.when(step == 1)
         def _():
-            arrive(0, 1, 0, half)
-            second_pushes[0].start()
-            arrive(1, 2, half, half)
-            second_pushes[1].start()
             lax.fori_loop(0, reps, turn, 0)
             pltpu.make_async_copy(off_all, off_hbm, out_sem.at[0]).start()
+            arrive(0, 1, 0, half)
+            later_pushes[6].start()
+            to_sibling(1, 0).start()
+            arrive(1, 2, half, half)
+            later_pushes[7].start()
+            to_sibling(2, 1).start()
             arrive(2, 3, 0, half)
+            to_sibling(3, 0).start()
+            backward(0)
+            arrive(3, 1, half, half)
+            to_sibling(1, 1).start()
+            later_pushes[8].start()
+            arrive(4, 2, 0, half)
+            later_pushes[10].start()
+            to_sibling(2, 0).start()
             arrive(5, 3, half, half)
-            second_pushes[2].start()
-            second_pushes[3].start()
-            arrive(3, 1, half, half)
-            to_sibling(1).start()
-            arrive(4, 2, 0, half)
-            to_sibling(2).start()
-            to_sibling(3).start()
+            later_pushes[9].start()
+            later_pushes[11].start()
+            to_sibling(3, 1).start()
 
         @pl.when(step == 2)
         def _():
             arrive(6, 4, 0, half)
-            third_pushes[0].start()
+            later_pushes[12].start()
+            to_sibling(4, 0).start()
             arrive(7, 4, half, half)
-            third_pushes[1].start()
-            to_sibling(4).start()
+            to_sibling(4, 1).start()
+
+        @pl.when(step == 4)
+        def _():
+            arrive(8, 5, 0, half)
+            to_sibling(5, 0).start()
+            arrive(9, 5, half, half)
+            later_pushes[13].start()
+            to_sibling(5, 1).start()
 
         @pl.when(step == 5)
         def _():
-            lax.fori_loop(0, 4, backward_step, 0)
-            arrive(8, 5, 0, share)
-            to_sibling(5).start()
-            arrive(9, 6, 0, share)
-            to_sibling(6).start()
-            arrive(10, 7, 0, half)
-            arrive(11, 7, half, half)
-            to_sibling(7).start()
-            lax.fori_loop(4, 5, backward_step, 0)
-
-        from_sibling(step)
+            arrive(10, 6, 0, half)
+            to_sibling(6, 0).start()
+            arrive(11, 6, half, half)
+            to_sibling(6, 1).start()
+
+        @pl.when(step == 7)
+        def _():
+            arrive(12, 7, 0, half)
+            to_sibling(7, 0).start()
+            lax.fori_loop(1, 3, backward_step, 0)
+            arrive(13, 7, half, half)
+            to_sibling(7, 1).start()
+            lax.fori_loop(3, 4, backward_step, 0)
+
+        from_sibling(step, 0)
+        from_sibling(step, 1)
         mom_copy(step).wait()
         forward(step)
         for ahead in range(1, reps):
@@ -316,12 +336,13 @@
         return carry
 
     lax.fori_loop(0, chips, one, 0)
-    lax.fori_loop(5, chips, backward_step, 0)
-    for copy in first_pushes + second_pushes + third_pushes:
+    lax.fori_loop(4, chips, backward_step, 0)
+    for copy in first_pushes + list(later_pushes.values()):
         copy.wait_send()
 
     def settle(step, carry):
-        to_sibling(step).wait_send()
+        to_sibling(step, 0).wait_send()
+        to_sibling(step, 1).wait_send()
         for behind in range(1, reps):
             take_values(step, behind).wait_recv()
         pltpu.make_async_copy(val_all.at[:, step], val_hbm.at[:, chip_of(step)], out_sem.at[1 + step]).start()
@@ -380,52 +401,78 @@
         new[rows, :] = (moved_ref[rows, :] - taken).astype(BF)
 
 
-def update_kernel(val_ref, off_ref, col_ref, spread_ref, seg_ref, new_in, up_ref, new_out, vals, sums, high_ref, low_ref):
-    step = pl.program_id(0)
+def update_kernel(val_hbm, off_hbm, col_hbm, spread_hbm, seg_hbm, new_in, up_hbm, new_out,
+                  val_ref, off_ref, col_ref, spread_ref, seg_ref, new, up, vals, sums, high_ref, low_ref,
+                  small_sem, in_sem, keep_sem, up_sem):
     groups, blocks = off_ref.shape[:2]
     chips = val_ref.shape[1]
-    new_out[...] = new_in[...]
-
-    @pl.when(step == 0)
-    def _():
-        for r in range(groups):
-            line = jnp.concatenate([val_ref[r, c][:, :FIVE * HALF] for c in range(chips)], axis=1)
-            for i in range(line.shape[1] // LANES):
-                vals[i, r] = line[:, i * LANES:(i + 1) * LANES]
-
-    column = lax.broadcasted_iota(jnp.int32, (BLOCK, LANES), 0).astype(F32)
-    powers = []
-    for b in range(blocks):
-        even = odd = jnp.zeros((BLOCK, LANES), F32)
-        for r in range(groups):
-            line = off_ref[r, b, pl.ds(step, 1), :]
-            val = jnp.broadcast_to(vals[step, r, b:b + 1, :], (BLOCK, LANES))
-            even = even + jnp.where(jnp.broadcast_to(line, (BLOCK, LANES)) == column, val, 0.0)
-            odd = odd + jnp.where(jnp.broadcast_to(line - BLOCK, (BLOCK, LANES)) == column, val, 0.0)
-        sums[b, :, :LANES] = even
-        sums[b, :, LANES:] = odd
-        powers.append(jnp.sum(even * even + odd * odd, axis=0, keepdims=True))
-    powers = jnp.concatenate(powers + [jnp.zeros((16 - blocks, LANES), F32)], axis=0)
-    high, low = split(powers)
-    power = dot(jnp.concatenate([high, low], axis=1), seg_ref[...])
-    scale = lax.rsqrt(power * (1.0 / (BLOCK * BLOCK)) + EPSILON)
-    for b in range(blocks):
-        row = jnp.concatenate([scale[b:b + 1]] * 2, axis=1)
-        high, low = split(sums[b] * row)
-        half = dot(col_ref[...], jnp.concatenate([high, low, high], axis=0))
-        high, low = split(half)
-        high_ref[b * BLOCK:(b + 1) * BLOCK, :] = high
-        low_ref[b * BLOCK:(b + 1) * BLOCK, :] = low
+    steps = vals.shape[0]
     rows = QUAD * BLOCK
-    width = high_ref.shape[0]
-    for start in range(0, width, 256):
-        cut = slice(start, min(start + 256, width))
-        field = dot_t(spread_ref[:rows], high_ref[cut]) + dot_t(spread_ref[rows:], high_ref[cut]) + dot_t(spread_ref[:rows], low_ref[cut])
-        up_ref[:, cut] = field.astype(BF)
-
-
-def whole(shape):
-    return pl.BlockSpec(shape, lambda i: (0,) * len(shape))
+    smalls = [pltpu.make_async_copy(a, b, small_sem.at[n]) for n, (a, b) in enumerate((
+        (val_hbm, val_ref), (off_hbm, off_ref), (seg_hbm, seg_ref), (col_hbm, col_ref), (spread_hbm, spread_ref)))]
+    for copy in smalls:
+        copy.start()
+
+    def piece(ref, step):
+        return ref.at[pl.ds(pl.multiple_of(step * rows, rows), rows), :]
+
+    def bring(step):
+        return pltpu.make_async_copy(piece(new_in, step), piece(new, step), in_sem.at[step])
+
+    def keep(step):
+        return pltpu.make_async_copy(piece(new, step), piece(new_out, step), keep_sem.at[step])
+
+    def hand_out(step):
+        return pltpu.make_async_copy(piece(up, step), piece(up_hbm, step), up_sem.at[step])
+
+    for step in range(steps):
+        bring(step).start()
+    smalls[0].wait()
+    for r in range(groups):
+        line = jnp.concatenate([val_ref[r, c][:, :FIVE * HALF] for c in range(chips)], axis=1)
+        for i in range(steps):
+            vals[i, r] = line[:, i * LANES:(i + 1) * LANES]
+    for copy in smalls[1:]:
+        copy.wait()
+
+    def one(step, carry):
+        bring(step).wait()
+        keep(step).start()
+        column = lax.broadcasted_iota(jnp.int32, (BLOCK, LANES), 0).astype(F32)
+        powers = []
+        for b in range(blocks):
+            even = odd = jnp.zeros((BLOCK, LANES), F32)
+            for r in range(groups):
+                line = off_ref[r, b, pl.ds(step, 1), :]
+                val = jnp.broadcast_to(vals[step, r, b:b + 1, :], (BLOCK, LANES))
+                even = even + jnp.where(jnp.broadcast_to(line, (BLOCK, LANES)) == column, val, 0.0)
+                odd = odd + jnp.where(jnp.broadcast_to(line - BLOCK, (BLOCK, LANES)) == column, val, 0.0)
+            sums[b, :, :LANES] = even
+            sums[b, :, LANES:] = odd
+            powers.append(jnp.sum(even * even + odd * odd, axis=0, keepdims=True))
+        powers = jnp.concatenate(powers + [jnp.zeros((16 - blocks, LANES), F32)], axis=0)
+        high, low = split(powers)
+        power = dot(jnp.concatenate([high, low], axis=1), seg_ref[...])
+        scale = lax.rsqrt(power * (1.0 / (BLOCK * BLOCK)) + EPSILON)
+        for b in range(blocks):
+            row = jnp.concatenate([scale[b:b + 1]] * 2, axis=1)
+            high, low = split(sums[b] * row)
+            half = dot(col_ref[...], jnp.concatenate([high, low, high], axis=0))
+            high, low = split(half)
+            high_ref[b * BLOCK:(b + 1) * BLOCK, :] = high
+            low_ref[b * BLOCK:(b + 1) * BLOCK, :] = low
+        width = high_ref.shape[0]
+        for start in range(0, width, 256):
+            cut = slice(start, min(start + 256, width))
+            field = dot_t(spread_ref[:rows], high_ref[cut]) + dot_t(spread_ref[rows:], high_ref[cut]) + dot_t(spread_ref[:rows], low_ref[cut])
+            up[pl.ds(pl.multiple_of(step * rows, rows), rows), cut] = field.astype(BF)
+        hand_out(step).start()
+        return carry
+
+    lax.fori_loop(0, steps, one, 0)
+    for step in range(steps):
+        keep(step).wait()
+        hand_out(step).wait()
 
 
 def gather_call(xt, g, mom, picks, t):
@@ -459,26 +506,33 @@
             pltpu.VMEM((chunks, HALF, LANES), F32),
             pltpu.VMEM(offsets, F32),
             pltpu.VMEM(values, F32),
-            dma((len(small),)), dma, dma((chunks,)), dma((chunks,)), dma((1 + chunks,)), dma, dma((12,)), dma((12,)), dma((chunks,)), dma((chunks,)), dma((chunks, reps)), dma((chunks, reps)),
+            dma((len(small),)), dma, dma((chunks,)), dma((chunks,)), dma((1 + chunks,)), dma, dma((14,)), dma((14,)), dma((chunks, 2)), dma((chunks, 2)), dma((chunks, reps)), dma((chunks, reps)),
         ],
         compiler_params=pltpu.CompilerParams(vmem_limit_bytes=56 * 2**20, collective_id=0, has_side_effects=True),
     )(xt, g, mom, *small)
 
 
 def update_call(values, off, new, t):
-    groups, chips = values.shape[:2]
-    blocks, steps = off.shape[1:3]
-    rows, width = QUAD * BLOCK, blocks * BLOCK
-    names = ("columns", "spread", "segment")
+    groups, blocks, steps = off.shape[:3]
+    width = blocks * BLOCK
+    small = [values, off] + [t[n] for n in ("columns", "spread", "segment")]
+    any_space, dma = pl.BlockSpec(memory_space=pl.ANY), pltpu.SemaphoreType.DMA
     return pl.pallas_call(
-        update_kernel, grid=(new.shape[0] // rows,),
-        in_specs=[whole(values.shape), whole(off.shape)] + [whole(t[n].shape) for n in names] + [pl.BlockSpec((rows, width), lambda i: (i, 0))],
-        out_specs=[pl.BlockSpec((rows, width), lambda i: (i, 0))] * 2,
-        out_shape=[jax.ShapeDtypeStruct(new.shape, BF), jax.ShapeDtypeStruct(new.shape, BF)],
-        scratch_shapes=[pltpu.VMEM((new.shape[0] // rows, groups, values.shape[2], LANES), F32),
-            pltpu.VMEM((blocks, BLOCK, 2 * LANES), F32), pltpu.VMEM((width, 2 * LANES), BF), pltpu.VMEM((width, 2 * LANES), BF)],
+        update_kernel,
+        in_specs=[any_space] * (len(small) + 1),
+        out_specs=[any_space] * 2,
+        out_shape=[jax.ShapeDtypeStruct(new.shape, BF)] * 2,
+        scratch_shapes=[pltpu.VMEM(a.shape, a.dtype) for a in small] + [
+            pltpu.VMEM(new.shape, BF),
+            pltpu.VMEM(new.shape, BF),
+            pltpu.VMEM((steps, groups, LISTED, LANES), F32),
+            pltpu.VMEM((blocks, BLOCK, 2 * LANES), F32),
+            pltpu.VMEM((width, 2 * LANES), BF),
+            pltpu.VMEM((width, 2 * LANES), BF),
+            dma((len(small),)), dma((steps,)), dma((steps,)), dma((steps,)),
+        ],
         compiler_params=pltpu.CompilerParams(vmem_limit_bytes=60 * 2**20),
-    )(values, off, *(t[n] for n in names), new)
+    )(*small, new)
 
 
 def body(tokens, output_grads, momentum, component_picks):

time: 67.7 us -> 66.7 us (0.985)
  Pallas kernels: 67 us -> 66 us
    pallas_call x1, Pallas kernels: 45.7 us -> 44.3 us  [gather_call(): pl.pallas_call(gather_kernel, in_specs=[any_space] * (3 + len(small)), ou...]
where the time goes in v5:
time: 66.7 us; the launch traced here: 66.6 us
  Pallas kernels  66 us (99%)
    pallas_call x1, Pallas kernels, gather_call(): pl.pallas_call(gather_kernel, in_specs=[any_space] * (3 + len(small)), ou...  44.3 us
    pallas_call x1, Pallas kernels, update_call(): pl.pallas_call(update_kernel, in_specs=[any_space] * (len(small) + 1), ou...  21.7 us

profile of v5, /device:TPU:1, one launch (start us, length us, event | category | flops | bytes accessed | tf_op | source)
XLA Modules:
  0.0 66.6 jit_solution(8492825767259433852)
XLA Ops:
  0.6 44.3 %shard_map.149 = (bf16[2560,896]{1,0:T(8,128)(2,1)}, f32[8,8,16,256]{3,2,1,0:T(8,128)}, f32[8,14,10,128]{3,2,1,0:T(8,128)}) custom-call(bf16[160,1024]{1,0:T(8,128)(2,1)} %bitcast.6, bf16[1024,896]{1,0:T(8,128)(2,1)} %g_hbm.1, bf16[2560,896]{1,0:T(8,128)(2,1)} %bitcast.4, s32[8,14,32,40]{3,2,1,0:T(8,128)} %bitcast.5, ...), custom_call_target="tpu_custom_call" | custom-call | tf_op jit(solution)/shard_map/pallas_call | solution.py:487
  44.9 21.7 %shard_map.150 = (bf16[2560,896]{1,0:T(8,128)(2,1)}, bf16[2560,896]{1,0:T(8,128)(2,1)}) custom-call(f32[8,8,16,256]{3,2,1,0:T(8,128)} %get-tuple-element.7.val_hbm, f32[8,14,10,128]{3,2,1,0:T(8,128)} %get-tuple-element.8.off_hbm, bf16[64,192]{1,0:T(8,128)(2,1)} %constant.27.clone.col_hbm, bf16[512,256]{1,0:T(8,128)(2,1)} %constant.28.clone.spread_hbm, ...), custom_call_target="tpu_custom_call" | custom-call | tf_op jit(solution)/shard_map/pallas_call | solution.py:520

commit v6 on v5

--- a/solution.py
+++ b/solution.py
@@ -65,7 +65,7 @@
     spread = np.zeros((QUAD, BLOCK, 2, QUAD, HALF))
     for p in range(QUAD):
         for parity in range(2):
-            spread[p, :, parity, p, :] = cosine[parity::2].T
+            spread[p, :, parity, p, :] = 0.5 * (cosine[0::2] + (1 - 2 * parity) * cosine[1::2]).T
     high, low = split_table(spread.reshape(QUAD * BLOCK, 2 * QUAD * HALF))
     segment = (np.arange(LANES)[:, None] // HALF == np.arange(LANES)[None, :] // HALF).astype(ml_dtypes.bfloat16)
     return {
@@ -77,7 +77,7 @@
         "expand": expand,
         "compress": (np.arange(LISTED)[:, None] == block).astype(ml_dtypes.bfloat16),
         "columns": columns,
-        "spread": np.concatenate([high, low]),
+        "spread": np.concatenate([high, high, low], axis=1),
         "segment": np.concatenate([segment, segment]),
     }
 
@@ -402,7 +402,7 @@
 
 
 def update_kernel(val_hbm, off_hbm, col_hbm, spread_hbm, seg_hbm, new_in, up_hbm, new_out,
-                  val_ref, off_ref, col_ref, spread_ref, seg_ref, new, up, vals, sums, high_ref, low_ref,
+                  val_ref, off_ref, col_ref, spread_ref, seg_ref, new, up, vals, sums, half_ref,
                   small_sem, in_sem, keep_sem, up_sem):
     groups, blocks = off_ref.shape[:2]
     chips = val_ref.shape[1]
@@ -425,8 +425,6 @@
     def hand_out(step):
         return pltpu.make_async_copy(piece(up, step), piece(up_hbm, step), up_sem.at[step])
 
-    for step in range(steps):
-        bring(step).start()
     smalls[0].wait()
     for r in range(groups):
         line = jnp.concatenate([val_ref[r, c][:, :FIVE * HALF] for c in range(chips)], axis=1)
@@ -436,36 +434,39 @@
         copy.wait()
 
     def one(step, carry):
-        bring(step).wait()
-        keep(step).start()
-        column = lax.broadcasted_iota(jnp.int32, (BLOCK, LANES), 0).astype(F32)
+        bring(step).start()
+        shape = (BLOCK // 8, 8, LANES)
+        column = (lax.broadcasted_iota(jnp.int32, shape, 0) * 8 + lax.broadcasted_iota(jnp.int32, shape, 1)).astype(F32)
         powers = []
         for b in range(blocks):
-            even = odd = jnp.zeros((BLOCK, LANES), F32)
+            total = signed = jnp.zeros(shape, F32)
             for r in range(groups):
-                line = off_ref[r, b, pl.ds(step, 1), :]
-                val = jnp.broadcast_to(vals[step, r, b:b + 1, :], (BLOCK, LANES))
-                even = even + jnp.where(jnp.broadcast_to(line, (BLOCK, LANES)) == column, val, 0.0)
-                odd = odd + jnp.where(jnp.broadcast_to(line - BLOCK, (BLOCK, LANES)) == column, val, 0.0)
-            sums[b, :, :LANES] = even
-            sums[b, :, LANES:] = odd
-            powers.append(jnp.sum(even * even + odd * odd, axis=0, keepdims=True))
+                off = jnp.broadcast_to(off_ref[r, b, pl.ds(step, 1), :], (8, LANES))
+                val = jnp.broadcast_to(vals[step, r, b:b + 1, :], (8, LANES))
+                odd = off >= BLOCK
+                place = jnp.where(odd, off - BLOCK, off)[None] == column
+                total = total + jnp.where(place, val[None], 0.0)
+                signed = signed + jnp.where(place, jnp.where(odd, -val, val)[None], 0.0)
+            sums[b, :, :LANES] = total.reshape(BLOCK, LANES)
+            sums[b, :, LANES:] = signed.reshape(BLOCK, LANES)
+            powers.append(jnp.sum(jnp.sum(total * total + signed * signed, axis=0), axis=0, keepdims=True))
         powers = jnp.concatenate(powers + [jnp.zeros((16 - blocks, LANES), F32)], axis=0)
         high, low = split(powers)
         power = dot(jnp.concatenate([high, low], axis=1), seg_ref[...])
-        scale = lax.rsqrt(power * (1.0 / (BLOCK * BLOCK)) + EPSILON)
+        scale = lax.rsqrt(power * (0.5 / (BLOCK * BLOCK)) + EPSILON)
         for b in range(blocks):
             row = jnp.concatenate([scale[b:b + 1]] * 2, axis=1)
             high, low = split(sums[b] * row)
             half = dot(col_ref[...], jnp.concatenate([high, low, high], axis=0))
             high, low = split(half)
-            high_ref[b * BLOCK:(b + 1) * BLOCK, :] = high
-            low_ref[b * BLOCK:(b + 1) * BLOCK, :] = low
-        width = high_ref.shape[0]
+            half_ref[b * BLOCK:(b + 1) * BLOCK, :] = jnp.concatenate([high, low, high], axis=1)
+        width = half_ref.shape[0]
         for start in range(0, width, 256):
             cut = slice(start, min(start + 256, width))
-            field = dot_t(spread_ref[:rows], high_ref[cut]) + dot_t(spread_ref[rows:], high_ref[cut]) + dot_t(spread_ref[:rows], low_ref[cut])
+            field = dot_t(spread_ref[...], half_ref[cut])
             up[pl.ds(pl.multiple_of(step * rows, rows), rows), cut] = field.astype(BF)
+        bring(step).wait()
+        keep(step).start()
         hand_out(step).start()
         return carry
 
@@ -527,8 +528,7 @@
             pltpu.VMEM(new.shape, BF),
             pltpu.VMEM((steps, groups, LISTED, LANES), F32),
             pltpu.VMEM((blocks, BLOCK, 2 * LANES), F32),
-            pltpu.VMEM((width, 2 * LANES), BF),
-            pltpu.VMEM((width, 2 * LANES), BF),
+            pltpu.VMEM((width, 6 * LANES), BF),
             dma((len(small),)), dma((steps,)), dma((steps,)), dma((steps,)),
         ],
         compiler_params=pltpu.CompilerParams(vmem_limit_bytes=60 * 2**20),

time: 66.7 us -> 64.9 us (0.973)
  Pallas kernels: 66 us -> 64.1 us
    pallas_call x1, Pallas kernels: 21.7 us -> 19.9 us  [update_call(): pl.pallas_call(update_kernel, in_specs=[any_space] * (len(small) + 1), ou...]
where the time goes in v6:
time: 64.9 us; the launch traced here: 64.7 us
  Pallas kernels  64.1 us (99%)
    pallas_call x1, Pallas kernels, gather_call(): pl.pallas_call(gather_kernel, in_specs=[any_space] * (3 + len(small)), ou...  44.3 us
    pallas_call x1, Pallas kernels, update_call(): pl.pallas_call(update_kernel, in_specs=[any_space] * (len(small) + 1), ou...  19.9 us

profile of v6, /device:TPU:1, one launch (start us, length us, event | category | flops | bytes accessed | tf_op | source)
XLA Modules:
  0.0 64.7 jit_solution(9656447978714382549)
XLA Ops:
  0.6 44.3 %shard_map.149 = (bf16[2560,896]{1,0:T(8,128)(2,1)}, f32[8,8,16,256]{3,2,1,0:T(8,128)}, f32[8,14,10,128]{3,2,1,0:T(8,128)}) custom-call(bf16[160,1024]{1,0:T(8,128)(2,1)} %bitcast.6, bf16[1024,896]{1,0:T(8,128)(2,1)} %g_hbm.1, bf16[2560,896]{1,0:T(8,128)(2,1)} %bitcast.4, s32[8,14,32,40]{3,2,1,0:T(8,128)} %bitcast.5, ...), custom_call_target="tpu_custom_call" | custom-call | tf_op jit(solution)/shard_map/pallas_call | solution.py:488
  44.9 19.9 %shard_map.150 = (bf16[2560,896]{1,0:T(8,128)(2,1)}, bf16[2560,896]{1,0:T(8,128)(2,1)}) custom-call(f32[8,8,16,256]{3,2,1,0:T(8,128)} %get-tuple-element.7.val_hbm, f32[8,14,10,128]{3,2,1,0:T(8,128)} %get-tuple-element.8.off_hbm, bf16[64,192]{1,0:T(8,128)(2,1)} %constant.27.clone.col_hbm, bf16[256,768]{1,0:T(8,128)(2,1)} %constant.28.clone.spread_hbm, ...), custom_call_target="tpu_custom_call" | custom-call | tf_op jit(solution)/shard_map/pallas_call | solution.py:521

commit v7 on v6

--- a/solution.py
+++ b/solution.py
@@ -273,29 +273,29 @@
     def one(step, carry):
         @pl.when(step == 1)
         def _():
-            lax.fori_loop(0, reps, turn, 0)
-            pltpu.make_async_copy(off_all, off_hbm, out_sem.at[0]).start()
             arrive(0, 1, 0, half)
-            later_pushes[6].start()
             to_sibling(1, 0).start()
             arrive(1, 2, half, half)
-            later_pushes[7].start()
             to_sibling(2, 1).start()
             arrive(2, 3, 0, half)
             to_sibling(3, 0).start()
-            backward(0)
+            lax.fori_loop(0, reps, turn, 0)
+            pltpu.make_async_copy(off_all, off_hbm, out_sem.at[0]).start()
+            later_pushes[6].start()
+            later_pushes[7].start()
             arrive(3, 1, half, half)
             to_sibling(1, 1).start()
             later_pushes[8].start()
             arrive(4, 2, 0, half)
+            to_sibling(2, 0).start()
             later_pushes[10].start()
-            to_sibling(2, 0).start()
             arrive(5, 3, half, half)
+            to_sibling(3, 1).start()
             later_pushes[9].start()
             later_pushes[11].start()
-            to_sibling(3, 1).start()
-
-        @pl.when(step == 2)
+            backward(0)
+
+        @pl.when(step == 3)
         def _():
             arrive(6, 4, 0, half)
             later_pushes[12].start()
@@ -307,25 +307,26 @@
         def _():
             arrive(8, 5, 0, half)
             to_sibling(5, 0).start()
+
+        @pl.when(step == 5)
+        def _():
             arrive(9, 5, half, half)
             later_pushes[13].start()
             to_sibling(5, 1).start()
-
-        @pl.when(step == 5)
-        def _():
             arrive(10, 6, 0, half)
             to_sibling(6, 0).start()
             arrive(11, 6, half, half)
             to_sibling(6, 1).start()
+            lax.fori_loop(1, 3, backward_step, 0)
 
         @pl.when(step == 7)
         def _():
             arrive(12, 7, 0, half)
             to_sibling(7, 0).start()
-            lax.fori_loop(1, 3, backward_step, 0)
+            lax.fori_loop(3, 4, backward_step, 0)
             arrive(13, 7, half, half)
             to_sibling(7, 1).start()
-            lax.fori_loop(3, 4, backward_step, 0)
+            lax.fori_loop(4, 5, backward_step, 0)
 
         from_sibling(step, 0)
         from_sibling(step, 1)
@@ -336,7 +337,7 @@
         return carry
 
     lax.fori_loop(0, chips, one, 0)
-    lax.fori_loop(4, chips, backward_step, 0)
+    lax.fori_loop(5, chips, backward_step, 0)
     for copy in first_pushes + list(later_pushes.values()):
         copy.wait_send()
 

time: 64.9 us -> 65.2 us (level)
  no operation moved by 1% of the time
where the time goes in v7:
time: 65.2 us; the launch traced here: 65.1 us
  Pallas kernels  64.4 us (99%)
    pallas_call x1, Pallas kernels, gather_call(): pl.pallas_call(gather_kernel, in_specs=[any_space] * (3 + len(small)), ou...  44.6 us
    pallas_call x1, Pallas kernels, update_call(): pl.pallas_call(update_kernel, in_specs=[any_space] * (len(small) + 1), ou...  19.9 us

profile of v7, /device:TPU:1, one launch (start us, length us, event | category | flops | bytes accessed | tf_op | source)
XLA Modules:
  0.0 65.1 jit_solution(9985081965849797275)
XLA Ops:
  0.6 44.6 %shard_map.149 = (bf16[2560,896]{1,0:T(8,128)(2,1)}, f32[8,8,16,256]{3,2,1,0:T(8,128)}, f32[8,14,10,128]{3,2,1,0:T(8,128)}) custom-call(bf16[160,1024]{1,0:T(8,128)(2,1)} %bitcast.6, bf16[1024,896]{1,0:T(8,128)(2,1)} %g_hbm.1, bf16[2560,896]{1,0:T(8,128)(2,1)} %bitcast.4, s32[8,14,32,40]{3,2,1,0:T(8,128)} %bitcast.5, ...), custom_call_target="tpu_custom_call" | custom-call | tf_op jit(solution)/shard_map/pallas_call | solution.py:489
  45.2 19.9 %shard_map.150 = (bf16[2560,896]{1,0:T(8,128)(2,1)}, bf16[2560,896]{1,0:T(8,128)(2,1)}) custom-call(f32[8,8,16,256]{3,2,1,0:T(8,128)} %get-tuple-element.7.val_hbm, f32[8,14,10,128]{3,2,1,0:T(8,128)} %get-tuple-element.8.off_hbm, bf16[64,192]{1,0:T(8,128)(2,1)} %constant.27.clone.col_hbm, bf16[256,768]{1,0:T(8,128)(2,1)} %constant.28.clone.spread_hbm, ...), custom_call_target="tpu_custom_call" | custom-call | tf_op jit(solution)/shard_map/pallas_call | solution.py:522

commit v8 on v6

--- a/solution.py
+++ b/solution.py
@@ -273,8 +273,6 @@
     def one(step, carry):
         @pl.when(step == 1)
         def _():
-            lax.fori_loop(0, reps, turn, 0)
-            pltpu.make_async_copy(off_all, off_hbm, out_sem.at[0]).start()
             arrive(0, 1, 0, half)
             later_pushes[6].start()
             to_sibling(1, 0).start()
@@ -283,6 +281,8 @@
             to_sibling(2, 1).start()
             arrive(2, 3, 0, half)
             to_sibling(3, 0).start()
+            lax.fori_loop(0, reps, turn, 0)
+            pltpu.make_async_copy(off_all, off_hbm, out_sem.at[0]).start()
             backward(0)
             arrive(3, 1, half, half)
             to_sibling(1, 1).start()

time: 64.9 us -> 65.2 us (level)
  no operation moved by 1% of the time
where the time goes in v8:
time: 65.2 us; the launch traced here: 65 us
  Pallas kernels  64.4 us (99%)
    pallas_call x1, Pallas kernels, gather_call(): pl.pallas_call(gather_kernel, in_specs=[any_space] * (3 + len(small)), ou...  44.5 us
    pallas_call x1, Pallas kernels, update_call(): pl.pallas_call(update_kernel, in_specs=[any_space] * (len(small) + 1), ou...  19.9 us

profile of v8, /device:TPU:1, one launch (start us, length us, event | category | flops | bytes accessed | tf_op | source)
XLA Modules:
  0.0 65.0 jit_solution(17827547804966294275)
XLA Ops:
  0.6 44.5 %shard_map.149 = (bf16[2560,896]{1,0:T(8,128)(2,1)}, f32[8,8,16,256]{3,2,1,0:T(8,128)}, f32[8,14,10,128]{3,2,1,0:T(8,128)}) custom-call(bf16[160,1024]{1,0:T(8,128)(2,1)} %bitcast.6, bf16[1024,896]{1,0:T(8,128)(2,1)} %g_hbm.1, bf16[2560,896]{1,0:T(8,128)(2,1)} %bitcast.4, s32[8,14,32,40]{3,2,1,0:T(8,128)} %bitcast.5, ...), custom_call_target="tpu_custom_call" | custom-call | tf_op jit(solution)/shard_map/pallas_call | solution.py:488
  45.2 19.9 %shard_map.150 = (bf16[2560,896]{1,0:T(8,128)(2,1)}, bf16[2560,896]{1,0:T(8,128)(2,1)}) custom-call(f32[8,8,16,256]{3,2,1,0:T(8,128)} %get-tuple-element.7.val_hbm, f32[8,14,10,128]{3,2,1,0:T(8,128)} %get-tuple-element.8.off_hbm, bf16[64,192]{1,0:T(8,128)(2,1)} %constant.27.clone.col_hbm, bf16[256,768]{1,0:T(8,128)(2,1)} %constant.28.clone.spread_hbm, ...), custom_call_target="tpu_custom_call" | custom-call | tf_op jit(solution)/shard_map/pallas_call | solution.py:521

commit v9 on v6

--- a/solution.py
+++ b/solution.py
@@ -283,7 +283,6 @@
             to_sibling(2, 1).start()
             arrive(2, 3, 0, half)
             to_sibling(3, 0).start()
-            backward(0)
             arrive(3, 1, half, half)
             to_sibling(1, 1).start()
             later_pushes[8].start()
@@ -322,7 +321,7 @@
         def _():
             arrive(12, 7, 0, half)
             to_sibling(7, 0).start()
-            lax.fori_loop(1, 3, backward_step, 0)
+            lax.fori_loop(0, 3, backward_step, 0)
             arrive(13, 7, half, half)
             to_sibling(7, 1).start()
             lax.fori_loop(3, 4, backward_step, 0)

time: 64.9 us -> 65.8 us (1.014)
  Pallas kernels: 64.1 us -> 65 us
    pallas_call x1, Pallas kernels: 44.3 us -> 45.1 us  [gather_call(): pl.pallas_call(gather_kernel, in_specs=[any_space] * (3 + len(small)), ou...]
where the time goes in v9:
time: 65.8 us; the launch traced here: 65.6 us
  Pallas kernels  65 us (99%)
    pallas_call x1, Pallas kernels, gather_call(): pl.pallas_call(gather_kernel, in_specs=[any_space] * (3 + len(small)), ou...  45.1 us
    pallas_call x1, Pallas kernels, update_call(): pl.pallas_call(update_kernel, in_specs=[any_space] * (len(small) + 1), ou...  19.9 us

profile of v9, /device:TPU:1, one launch (start us, length us, event | category | flops | bytes accessed | tf_op | source)
XLA Modules:
  0.0 65.6 jit_solution(14176902689707168613)
XLA Ops:
  0.6 45.1 %shard_map.149 = (bf16[2560,896]{1,0:T(8,128)(2,1)}, f32[8,8,16,256]{3,2,1,0:T(8,128)}, f32[8,14,10,128]{3,2,1,0:T(8,128)}) custom-call(bf16[160,1024]{1,0:T(8,128)(2,1)} %bitcast.6, bf16[1024,896]{1,0:T(8,128)(2,1)} %g_hbm.1, bf16[2560,896]{1,0:T(8,128)(2,1)} %bitcast.4, s32[8,14,32,40]{3,2,1,0:T(8,128)} %bitcast.5, ...), custom_call_target="tpu_custom_call" | custom-call | tf_op jit(solution)/shard_map/pallas_call | solution.py:487
  45.8 19.9 %shard_map.150 = (bf16[2560,896]{1,0:T(8,128)(2,1)}, bf16[2560,896]{1,0:T(8,128)(2,1)}) custom-call(f32[8,8,16,256]{3,2,1,0:T(8,128)} %get-tuple-element.7.val_hbm, f32[8,14,10,128]{3,2,1,0:T(8,128)} %get-tuple-element.8.off_hbm, bf16[64,192]{1,0:T(8,128)(2,1)} %constant.27.clone.col_hbm, bf16[256,768]{1,0:T(8,128)(2,1)} %constant.28.clone.spread_hbm, ...), custom_call_target="tpu_custom_call" | custom-call | tf_op jit(solution)/shard_map/pallas_call | solution.py:520
